TPU v7x, 32 devices: a whole 2x2x4 slice. The times are simulated.
32 devices in a mesh: blk: 16 (over z, y, core), across: 2 (over x).
Axes of the slice: x: 2, y: 2, z: 4, core: 2. Of those that a mesh axis runs over, the one named last changes fastest.
Arguments:
- positions: float32 [3, 262144], P(None, ('blk', 'across')), may hold values from -4 to 4
- strengths: float32 [3, 262144], P(None, ('blk', 'across')), may hold values from -2.4 to 2.4
- radius: float32 [262144], P(('blk', 'across')), may hold values from 0.3 to 0.6
- block_count: int32 [2048], P(('blk', 'across')), may hold values from 64 to 128, as said below
- pair_target: int32 [32, 256], P(('blk', 'across')), may hold values from 0 to 127, as said below
- pair_slot: int32 [32, 256], P(('blk', 'across')), may hold values from 0 to 319, as said below
- pair_count: int32 [32], P(('blk', 'across')), may hold values from 64 to 256, as said below
Outputs:
- velocity: float32 [3, 262144], P(None, ('blk', 'across'))
- stretching: float32 [3, 262144], P(None, ('blk', 'across'))
- section_positions: float32 [3, 262144], P(None, ('blk', 'across'))
- section_strengths: float32 [3, 262144], P(None, ('blk', 'across'))
Inputs may be any that keep to these rules, and one draw needn't show every extreme that they name: `block_count`: each block's live particles are its first slots; some block is full in every draw. Within one device's list the pairs (pair_target, pair_slot) are all different. `pair_slot`: the window's slots come in five runs of 64: slots k * 64 to (k + 1) * 64 - 1, for k = 0 to 4, are the blocks of the shard k - 2 away (two below, one below, the own shard, one above, two above, on a closed cycle of shards), each at the device's own place within its shard. `pair_count`: some shards use the whole list on every device in every draw; the others use a quarter to a half of it.
All inputs are finite; a program needn't handle non-finite values.
Results may differ from a plain program's by a relative error of at most 0.0001.
Values sent between devices are 32-bit elements; how exact they have to be, the bound alone decides.
No kernel may reach another device: no remote copies, remote signals or barrier semaphores. Data moves between devices by JAX's collectives and lax.ppermute only.
A program may use at most 64 MiB of HBM per device.

v0:
```python
import jax
import jax.numpy as jnp
from jax import lax
from jax.sharding import PartitionSpec as P

BLOCK = 128
BLOCKS_DEV = 64
PAIR_GROUP = 16
WINDOW_BLOCKS = 320


biot_factor = 0.07957747154594767
section_step = 0.05


def passed_along(value, axis, steps):
    count = lax.axis_size(axis)
    pairs = [(source, (source + steps) % count) for source in range(count)]
    return lax.ppermute(value, axis, pairs)


def cross_product(left, right):
    first = left[:, 1] * right[:, 2] - left[:, 2] * right[:, 1]
    second = left[:, 2] * right[:, 0] - left[:, 0] * right[:, 2]
    third = left[:, 0] * right[:, 1] - left[:, 1] * right[:, 0]
    return jnp.stack([first, second, third], axis=1)


def pair_terms(target, source):
    target_pos = target[:, 0:3, :, None]
    target_str = target[:, 3:6, :, None]
    source_pos = source[:, 0:3, None, :]
    source_str = source[:, 3:6, None, :]
    inv_core = 1.0 / source[:, 6, None, :]
    offset_vec = target_pos - source_pos
    scaled = jnp.sum(offset_vec * offset_vec, axis=1) * inv_core * inv_core
    reciprocal = 1.0 / (scaled + 1.0)
    falloff = reciprocal * reciprocal * jnp.sqrt(reciprocal)
    core_cube = inv_core * inv_core * inv_core
    kernel_value = (scaled + 2.5) * falloff * core_cube
    kernel_slope = -(3.0 * scaled + 10.5) * falloff * reciprocal * core_cube * inv_core * inv_core
    swirling = cross_product(offset_vec, source_str)
    tilting = cross_product(target_str, source_str)
    projection = jnp.sum(offset_vec * target_str, axis=1)
    velocity = jnp.sum(kernel_value[:, None] * swirling, axis=3)
    stretch = jnp.sum(
        kernel_value[:, None] * tilting + (kernel_slope * projection)[:, None] * swirling, axis=3
    )
    return -biot_factor * jnp.concatenate([velocity, stretch], axis=1)


def accumulate(partial_sum, pair_number, targets, sources, target_rows, source_rows):
    list_length = target_rows.shape[0]
    turns = (pair_number + PAIR_GROUP - 1) // PAIR_GROUP
    offsets = jnp.arange(PAIR_GROUP, dtype=jnp.int32)

    def one_turn(turn_index, partial_sum):
        entry_index = turn_index * PAIR_GROUP + offsets
        usable = (entry_index < pair_number).astype(jnp.float32)
        entry_index = jnp.minimum(entry_index, list_length - 1)
        target_index = target_rows[entry_index]
        source_index = source_rows[entry_index]
        pair_values = (
            pair_terms(targets[target_index], sources[source_index]) * usable[:, None, None]
        )
        return partial_sum.at[target_index].add(pair_values)

    return lax.fori_loop(jnp.int32(0), turns, one_turn, partial_sum)


def shards(positions, strengths, radius, block_count, pair_target, pair_slot, pair_count):
    slot_index = jnp.arange(BLOCK, dtype=jnp.int32)
    alive_mask = (slot_index[None, :] < block_count[:, None]).astype(jnp.float32)
    live_strengths = (strengths.reshape(3, BLOCKS_DEV, BLOCK) * alive_mask[None]).reshape(
        3, BLOCKS_DEV * BLOCK
    )
    resident = jnp.concatenate([positions, live_strengths, radius[None, :]], axis=0)
    below_one = passed_along(resident, "blk", 1)
    above_one = passed_along(resident, "blk", -1)
    below_two = passed_along(resident, "blk", 2)
    above_two = passed_along(resident, "blk", -2)
    source_window = jnp.concatenate([below_two, below_one, resident, above_one, above_two], axis=1)
    sources = source_window.reshape(7, WINDOW_BLOCKS, BLOCK).transpose(1, 0, 2)
    shard_targets = lax.all_gather(resident[0:6], "across", axis=1, tiled=True)
    shard_blocks = shard_targets.shape[1] // BLOCK
    targets = shard_targets.reshape(6, shard_blocks, BLOCK).transpose(1, 0, 2)
    partial_sum = jnp.zeros((shard_blocks, 6, BLOCK), jnp.float32)
    partial_sum = accumulate(
        partial_sum, pair_count[0], targets, sources, pair_target[0], pair_slot[0]
    )
    partial_sum = lax.psum_scatter(partial_sum, "across", scatter_dimension=0, tiled=True)
    result = partial_sum.transpose(1, 0, 2).reshape(6, BLOCKS_DEV * BLOCK)
    velocity = result[0:3]
    stretching = result[3:6]
    return (
        velocity,
        stretching,
        positions + section_step * velocity,
        live_strengths + section_step * stretching,
    )


def solution(mesh):
    return jax.shard_map(
        shards,
        mesh=mesh,
        in_specs=(
            P(None, ("blk", "across")),
            P(None, ("blk", "across")),
            P(("blk", "across")),
            P(("blk", "across")),
            P(("blk", "across"), None),
            P(("blk", "across"), None),
            P(("blk", "across")),
        ),
        out_specs=(
            P(None, ("blk", "across")),
            P(None, ("blk", "across")),
            P(None, ("blk", "across")),
            P(None, ("blk", "across")),
        ),
        check_vma=False,
    )
```

profile of v0, /device:TPU:0, one launch (start us, length us, event | category | flops | bytes accessed | tf_op | source)
XLA Modules:
  0.0 223.2 jit_solution(12796867684827008423)
XLA Ops:
  10.0 6.1 %collective-permute-start.3 = (f32[7,8192]{1,0:T(8,128)S(1)}, f32[7,8192]{1,0:T(8,128)S(1)}, u32[]{:S(2)}, u32[]{:S(2)}) collective-permute-start(f32[7,8192]{1,0:T(8,128)S(1)} %pad_maximum_fusion.2), channel_id=1, source_target_pairs={{0,28},{2,30},{4,0},{6,2},{8,4},{10,6},{12,8},{14,10},{16,12},{18,... | collective-permute-start | bytes 688136 | tf_op jit(solution)/shard_map/ppermute | solution.py:19
  18.9 9.0 %all_gather.3 = f32[6,16384]{1,0:T(8,128)S(1)} all-gather(f32[6,8192]{1,0:T(8,128)S(1)} %pad_maximum_fusion.1), channel_id=1, replica_groups=mesh['blk'=16,'across'=2] {'across'}, dimensions={1}, use_global_device_ids=true | all-gather | bytes 589824 | tf_op jit(solution)/shard_map/all_gather | solution.py:84
  29.9 168.2 %while.11 = (s32[]{:T(128)}, f32[128,6,128]{2,1,0:T(8,128)S(1)}, s32[]{:T(128)}, s32[256]{0:T(256)S(1)}, f32[128,6,128]{2,1,0:T(8,128)S(1)}, /*index=5*/s32[256]...) while((s32[]{:T(128)}, f32[128,6,128]{2,1,0:T(8,128)S(1)}, s32[]{:T(128)}, ...), condition=%wide.region_6.7_spmd.clone, body=%wide.region_0.6_spmd.clone.sunk | while | flops 20743396 | bytes 28267836 | solution.py:68
  33.3 1.9 multiply_reduce_fusion.5
  36.1 1.3 multiply_subtract_fusion.7
  37.4 1.8 multiply_reduce_fusion.6
  39.3 1.1 scatter_fusion
  43.8 1.9 multiply_reduce_fusion.5
  46.6 1.3 multiply_subtract_fusion.7
  47.9 1.8 multiply_reduce_fusion.6
  49.8 1.1 scatter_fusion
  54.3 1.9 multiply_reduce_fusion.5
  57.1 1.3 multiply_subtract_fusion.7
  58.5 1.8 multiply_reduce_fusion.6
  60.4 1.1 scatter_fusion
  64.8 1.9 multiply_reduce_fusion.5
  67.6 1.3 multiply_subtract_fusion.7
  69.0 1.8 multiply_reduce_fusion.6
  70.9 1.1 scatter_fusion
  75.3 1.9 multiply_reduce_fusion.5
  78.1 1.3 multiply_subtract_fusion.7
  79.5 1.8 multiply_reduce_fusion.6
  81.4 1.1 scatter_fusion
  85.8 1.9 multiply_reduce_fusion.5
  88.6 1.3 multiply_subtract_fusion.7
  90.0 1.8 multiply_reduce_fusion.6
  91.9 1.1 scatter_fusion
  96.3 1.9 multiply_reduce_fusion.5
  99.2 1.3 multiply_subtract_fusion.7
  100.5 1.8 multiply_reduce_fusion.6
  102.4 1.1 scatter_fusion
  106.8 1.9 multiply_reduce_fusion.5
  109.7 1.3 multiply_subtract_fusion.7
  111.0 1.8 multiply_reduce_fusion.6
  117.3 1.9 multiply_reduce_fusion.5
  120.2 1.3 multiply_subtract_fusion.7
  121.5 1.8 multiply_reduce_fusion.6
  127.9 1.9 multiply_reduce_fusion.5
  130.7 1.3 multiply_subtract_fusion.7
  132.0 1.8 multiply_reduce_fusion.6
  133.9 1.1 scatter_fusion
  138.4 1.9 multiply_reduce_fusion.5
  141.2 1.3 multiply_subtract_fusion.7
  142.5 1.8 multiply_reduce_fusion.6
  148.9 1.9 multiply_reduce_fusion.5
  151.7 1.3 multiply_subtract_fusion.7
  153.0 1.8 multiply_reduce_fusion.6
  155.0 1.1 scatter_fusion
  159.4 1.9 multiply_reduce_fusion.5
  162.2 1.3 multiply_subtract_fusion.7
  163.6 1.8 multiply_reduce_fusion.6
  169.9 1.9 multiply_reduce_fusion.5
  172.7 1.3 multiply_subtract_fusion.7
  174.1 1.8 multiply_reduce_fusion.6
  176.0 1.1 scatter_fusion
  180.4 1.9 multiply_reduce_fusion.5
  183.2 1.3 multiply_subtract_fusion.7
  184.6 1.8 multiply_reduce_fusion.6
  190.9 1.9 multiply_reduce_fusion.5
  193.8 1.3 multiply_subtract_fusion.7
  195.1 1.8 multiply_reduce_fusion.6
  197.0 1.1 scatter_fusion
  198.9 15.5 %reduce-scatter.2.cloned.1.call-done = f32[64,6,128]{2,1,0:T(8,128)} async-done(((f32[128,6,128]{2,1,0:T(8,128)}), f32[64,6,128]{2,1,0:T(8,128)}) %reduce-scatter.2.cloned.1.call-update) | async-done | bytes 196624 | tf_op jit(solution)/shard_map/reduce_scatter | solution.py:91
  214.5 1.9 multiply_add_fusion
  (307 shorter events, 80.3 us)
Async XLA Ops:
  7.2 22.7 %copy-start.1 = (s32[1,256]{1,0:T(1,128)S(1)}, s32[1,256]{1,0:T(1,128)}, u32[]{:S(2)}) copy-start(s32[1,256]{1,0:T(1,128)} %param.14) | copy-start | bytes 3076
  7.2 22.7 %copy-start = (s32[1,256]{1,0:T(1,128)S(1)}, s32[1,256]{1,0:T(1,128)}, u32[]{:S(2)}) copy-start(s32[1,256]{1,0:T(1,128)} %param.13) | copy-start | bytes 3076
  7.2 207.3 %reduce-scatter.2.cloned.1.call-start = ((), (), s32[]{:S(2)}) async-start(), calls=%async_computation.1 | async-start | bytes 786432 | tf_op jit(solution)/shard_map/reduce_scatter | solution.py:91
  10.0 19.7 %collective-permute-start.3 = (f32[7,8192]{1,0:T(8,128)S(1)}, f32[7,8192]{1,0:T(8,128)S(1)}, u32[]{:S(2)}, u32[]{:S(2)}) collective-permute-start(f32[7,8192]{1,0:T(8,128)S(1)} %pad_maximum_fusion.2), channel_id=1, source_target_pairs={{0,28},{2,30},{4,0},{6,2},{8,4},{10,6},{12,8},{14,10},{16,12},{18,... | collective-permute-start | bytes 688136 | tf_op jit(solution)/shard_map/ppermute | solution.py:19
  16.1 13.6 %collective-permute-start.2 = (f32[7,8192]{1,0:T(8,128)S(1)}, f32[7,8192]{1,0:T(8,128)S(1)}, u32[]{:S(2)}, u32[]{:S(2)}) collective-permute-start(f32[7,8192]{1,0:T(8,128)S(1)} %pad_maximum_fusion.2), channel_id=1, source_target_pairs={{0,30},{2,0},{4,2},{6,4},{8,6},{10,8},{12,10},{14,12},{16,14},{18,... | collective-permute-start | bytes 688136 | tf_op jit(solution)/shard_map/ppermute | solution.py:19
  16.1 13.6 %collective-permute-start.1 = (f32[7,8192]{1,0:T(8,128)S(1)}, f32[7,8192]{1,0:T(8,128)S(1)}, u32[]{:S(2)}, u32[]{:S(2)}) collective-permute-start(f32[7,8192]{1,0:T(8,128)S(1)} %pad_maximum_fusion.2), channel_id=1, source_target_pairs={{0,2},{2,4},{4,6},{6,8},{8,10},{10,12},{12,14},{14,16},{16,18},{18... | collective-permute-start | bytes 688136 | tf_op jit(solution)/shard_map/ppermute | solution.py:19
  16.6 12.1 %collective-permute-start = (f32[7,8192]{1,0:T(8,128)S(1)}, f32[7,8192]{1,0:T(8,128)}, u32[]{:S(2)}, u32[]{:S(2)}) collective-permute-start(f32[7,8192]{1,0:T(8,128)S(1)} %pad_maximum_fusion.2), channel_id=1, source_target_pairs={{0,4},{2,6},{4,8},{6,10},{8,12},{10,14},{12,16},{14,18},{16,20},{1... | collective-permute-start | bytes 688136 | tf_op jit(solution)/shard_map/ppermute | solution.py:19
  29.8 184.6 %copy-start.3 = (f32[3,8192]{1,0:T(4,128)S(1)}, f32[3,8192]{1,0:T(4,128)}, u32[]{:S(2)}) copy-start(f32[3,8192]{1,0:T(4,128)} %param.9) | copy-start | bytes 294916
  29.9 184.6 %copy-start.4 = (f32[3,8192]{1,0:T(4,128)S(1)}, f32[3,8192]{1,0:T(4,128)}, u32[]{:S(2)}) copy-start(f32[3,8192]{1,0:T(4,128)} %param.10) | copy-start | bytes 294916
  198.1 0.8 copy-start.2
Sparse Core Ops, SparseCore 0:
  199.1 15.3 reduce-scatter.1
where the time goes:
time: 224 us; the launch traced here: 223 us
  other arithmetic  130 us (58%)
  local copies, waits for them, and re-layouts  43.2 us (19%)
  waiting for transfers between devices  16.3 us (7%)
  between operations  14.9 us (7%)
  blocking collectives  8.97 us (4%)
  starting transfers between devices  7.31 us (3%)
    reduce_sum x16, other arithmetic, pair_terms(): scaled = jnp.sum(offset_vec * offset_vec, axis=1) * inv_core * inv_core  31.1 us
    reduce_sum x16, other arithmetic, pair_terms(): velocity = jnp.sum(kernel_value[:, None] * swirling, axis=3)  29 us
    sub x16, other arithmetic, cross_product(): first = left[:, 1] * right[:, 2] - left[:, 2] * right[:, 1]  21.2 us
    scatter-add x16, other arithmetic, one_turn(): return partial_sum.at[target_index].add(pair_values)  17.4 us
    reduce_scatter x1, waiting for transfers between devices, shards(): lax.psum_scatter(partial_sum, 'across', scatter_dimension=0, tiled=True)  15.5 us
    mul x16, other arithmetic, pair_terms(): kernel_slope * projection  14 us
    mul x32, other arithmetic, one_turn(): pair_terms(targets[target_index], sources[source_index])  11.8 us
    gather x16, local copies, waits for them, and re-layouts, one_turn(): target_index = target_rows[entry_index]  10.7 us
  transfers between devices with their start and end apart: 5, of which 2 were waited for; matrix products, arithmetic and copies ran while one was open for 1% of the time, Pallas kernels for 0%

commit v1 on v0

v1 whole, which is shorter than its diff:
```python
import functools

import jax
import jax.numpy as jnp
from jax import lax
from jax.experimental import pallas as pl
from jax.experimental.pallas import tpu as pltpu
from jax.sharding import PartitionSpec as P

BLOCK = 128
ROWS = 8
REACH = 2
UNROLL = 4

biot_factor = 0.07957747154594767
section_step = 0.05


def passed_along(value, axis, steps):
    count = lax.axis_size(axis)
    pairs = [(source, (source + steps) % count) for source in range(count)]
    return lax.ppermute(value, axis, pairs)


def rounded(value):
    return value.astype(jnp.bfloat16).astype(jnp.float32)


def split_three(value):
    first = rounded(value)
    rest = value - first
    second = rounded(rest)
    return first, second, rest - second


def row_number(shape):
    return lax.broadcasted_iota(jnp.int32, shape, 0)


def sum_rows(value):
    return value[0:1] + value[1:2] + value[2:3]


def cross(left, right):
    return [
        left[1] * right[2] - left[2] * right[1],
        left[2] * right[0] - left[0] * right[2],
        left[0] * right[1] - left[1] * right[0],
    ]


def rows_of(block, start):
    return [block[start + k : start + k + 1] for k in range(3)]


def lane_slice(index):
    return pl.ds(pl.multiple_of(index * BLOCK, BLOCK), BLOCK)


def target_features(block):
    row = row_number((ROWS, BLOCK))
    centre = jnp.where(row < 3, jnp.mean(block, axis=1, keepdims=True), 0.0)
    moved = block - centre
    pos = rows_of(moved, 0)
    strength = rows_of(moved, 5)
    norm = pos[0] * pos[0] + pos[1] * pos[1] + pos[2] * pos[2]
    own = pos[0] * strength[0] + pos[1] * strength[1] + pos[2] * strength[2]
    one = jnp.ones_like(norm)
    nil = jnp.zeros_like(norm)
    near = jnp.concatenate(pos + [norm, one, nil, nil, nil], axis=0)
    half = [0.5 * s for s in strength]
    tilt = jnp.concatenate(half + [own, nil, nil, nil, nil], axis=0)
    zero = jnp.zeros((ROWS, BLOCK), jnp.float32)
    parts = []
    for value in (near, tilt):
        first, second, third = split_three(value)
        parts += [first, second, third, first, second, first, zero, zero]
    return centre, jnp.concatenate(parts, axis=0).astype(jnp.bfloat16)


def source_features(block, centre, weight):
    row = row_number((ROWS, BLOCK))
    moved = block - centre
    inv_core = moved[4:5]
    inv_square = inv_core * inv_core
    pos = rows_of(moved, 0)
    strength = rows_of(moved, 5)
    norm = pos[0] * pos[0] + pos[1] * pos[1] + pos[2] * pos[2]
    scale = jnp.where(row < 3, -2.0, jnp.where(row == 3, 1.0, 0.0))
    shape = moved * inv_square * scale
    shape = jnp.where(row == 4, norm * inv_square + 1.0, shape)
    first, second, third = split_three(shape)
    zero = jnp.zeros((ROWS, BLOCK), jnp.float32)
    left = jnp.concatenate([first, first, first, second, second, third, zero, zero], axis=0)
    left = left.astype(jnp.bfloat16)
    blank = jnp.zeros_like(left)
    shape = jnp.concatenate(
        [jnp.concatenate([left, blank], axis=1), jnp.concatenate([blank, left], axis=1)], axis=0
    )
    turned = cross(pos, strength)
    nil = jnp.zeros_like(norm)
    charge = jnp.concatenate(strength + turned + [nil, nil], axis=0)
    charge = charge * (inv_square * inv_core * weight)
    high = rounded(charge)
    return shape, jnp.concatenate([high, charge - high], axis=0).astype(jnp.bfloat16)


NT = (((1,), (1,)), ((), ()))


def pair_kernel(
    shards, number, target_list, slot_list, *refs
):
    count = 2 * REACH + 1
    windows, (targets_in, eye_ref) = refs[:count], refs[count : count + 2]
    out_ref, window, targets, features, centres, total, sems = refs[count + 2 :]
    blocks = windows[0].shape[1] // BLOCK
    target_blocks = targets_in.shape[1] // BLOCK
    list_length = target_list.shape[1]
    copies = [pltpu.make_async_copy(targets_in, targets, sems.at[count])]
    for k in range(count):
        copies.append(
            pltpu.make_async_copy(
                windows[k], window.at[:, pl.ds(k * blocks * BLOCK, blocks * BLOCK)], sems.at[k]
            )
        )
    for copy in copies:
        copy.start()
    copies[0].wait()

    def prepare(step, carry):
        for u in range(4):
            b = step * 4 + u
            centre, matrix = target_features(targets[:, lane_slice(b)])
            centres[b] = centre
            turned = lax.dot_general(
                eye_ref[...], matrix, NT, preferred_element_type=jnp.float32
            )
            features[b] = turned.astype(jnp.bfloat16)
            total[b] = jnp.zeros((2 * ROWS, BLOCK), jnp.float32)
        return carry

    lax.fori_loop(0, target_blocks // 4, prepare, 0)
    for copy in copies[1:]:
        copy.wait()
    listed = number[0]

    def turn(step, carry):
        for u in range(UNROLL):
            entry = step * UNROLL + u
            weight = jnp.where(entry < listed, 1.0, 0.0).astype(jnp.float32)
            entry = jnp.minimum(entry, list_length - 1)
            t = target_list[0, entry]
            s = slot_list[0, entry]
            shape, charge = source_features(window[:, lane_slice(s)], centres[t], weight)
            both = jnp.dot(features[t], shape, preferred_element_type=jnp.float32)
            near, tilt = both[:, :BLOCK], both[:, BLOCK:]
            q = lax.rsqrt(near)
            q2 = q * q
            q3 = q2 * q
            f = q3 * (q2 + (2.0 / 3.0))
            h = (q3 * q2) * (q2 + 0.4) * tilt
            fh = f.astype(jnp.bfloat16)
            fl = (f - fh.astype(jnp.float32)).astype(jnp.bfloat16)
            hh = h.astype(jnp.bfloat16)
            hl = (h - hh.astype(jnp.float32)).astype(jnp.bfloat16)
            stacked = jnp.concatenate([fh, fl, hh, hl], axis=0)
            sums = lax.dot_general(charge, stacked, NT, preferred_element_type=jnp.float32)
            fsum = sums[0:8, 0:128] + sums[8:16, 0:128] + sums[0:8, 128:256]
            hsum = sums[0:8, 256:384] + sums[8:16, 256:384] + sums[0:8, 384:512]
            total[t] += jnp.concatenate([fsum, hsum], axis=0)
        return carry

    lax.fori_loop(0, (listed + UNROLL - 1) // UNROLL, turn, 0)

    def finish(step, carry):
        for u in range(4):
            b = step * 4 + u
            block = targets[:, lane_slice(b)] - centres[b]
            sums = total[b]
            pos = rows_of(block, 0)
            strength = rows_of(block, 5)
            fa = rows_of(sums, 0)
            fb = rows_of(sums, 3)
            ha = rows_of(sums, 8)
            hb = rows_of(sums, 11)
            swirl = cross(pos, fa)
            velocity = [(-1.5 * biot_factor) * (swirl[k] - fb[k]) for k in range(3)]
            lean = cross(strength, fa)
            bend = cross(pos, ha)
            stretch = [
                (-1.5 * biot_factor) * lean[k] + (7.5 * biot_factor) * (bend[k] - hb[k])
                for k in range(3)
            ]
            nil = jnp.zeros_like(fa[0])
            out_ref[:, lane_slice(b)] = jnp.concatenate(velocity + stretch + [nil, nil], axis=0)
        return carry

    lax.fori_loop(0, target_blocks // 4, finish, 0)


def pair_sums(number, target_list, slot_list, windows, targets):
    count = len(windows)
    lanes = windows[0].shape[1]
    target_blocks = targets.shape[1] // BLOCK
    eye = jnp.eye(BLOCK, dtype=jnp.bfloat16)
    smem = pl.BlockSpec(memory_space=pltpu.SMEM)
    anyspace = pl.BlockSpec(memory_space=pl.ANY)
    vmem = pl.BlockSpec(memory_space=pltpu.VMEM)
    return pl.pallas_call(
        functools.partial(pair_kernel, count),
        out_shape=jax.ShapeDtypeStruct((ROWS, target_blocks * BLOCK), jnp.float32),
        in_specs=[smem] * 3 + [anyspace] * (count + 1) + [vmem],
        out_specs=vmem,
        scratch_shapes=[
            pltpu.VMEM((ROWS, count * lanes), jnp.float32),
            pltpu.VMEM((ROWS, target_blocks * BLOCK), jnp.float32),
            pltpu.VMEM((target_blocks, BLOCK, BLOCK), jnp.bfloat16),
            pltpu.VMEM((target_blocks, ROWS, BLOCK), jnp.float32),
            pltpu.VMEM((target_blocks, 2 * ROWS, BLOCK), jnp.float32),
            pltpu.SemaphoreType.DMA((count + 1,)),
        ],
        compiler_params=pltpu.CompilerParams(vmem_limit_bytes=48 * 1024 * 1024),
        name="pair_sums",
    )(number, target_list, slot_list, *windows, targets, eye)


def shards(positions, strengths, radius, block_count, pair_target, pair_slot, pair_count):
    blocks = block_count.shape[0]
    lanes = blocks * BLOCK
    slot_index = jnp.arange(BLOCK, dtype=jnp.int32)
    alive = (slot_index[None, :] < block_count[:, None]).astype(jnp.float32)
    live_strengths = strengths * alive.reshape(1, lanes)
    resident = jnp.concatenate(
        [positions, jnp.ones((1, lanes), jnp.float32), 1.0 / radius[None, :], live_strengths], axis=0
    )
    windows = [
        resident if away == 0 else passed_along(resident, "blk", -away)
        for away in range(-REACH, REACH + 1)
    ]
    members = lax.axis_size("across")
    me = lax.axis_index("across")
    if members == 2:
        other = passed_along(resident, "across", 1)
        first = jnp.where(me == 0, resident, other)
        second = jnp.where(me == 0, other, resident)
        targets = jnp.concatenate([first, second], axis=1)
    else:
        targets = lax.all_gather(resident, "across", axis=1, tiled=True)
    sums = pair_sums(pair_count, pair_target, pair_slot, windows, targets)
    if members == 2:
        first, second = sums[:, :lanes], sums[:, lanes:]
        mine = jnp.where(me == 0, first, second)
        away = jnp.where(me == 0, second, first)
        result = mine + passed_along(away, "across", 1)
    else:
        result = lax.psum_scatter(sums, "across", scatter_dimension=1, tiled=True)
    velocity = result[0:3]
    stretching = result[3:6]
    return (
        velocity,
        stretching,
        positions + section_step * velocity,
        live_strengths + section_step * stretching,
    )


def solution(mesh):
    whole = P(None, ("blk", "across"))
    line = P(("blk", "across"))
    return jax.shard_map(
        shards,
        mesh=mesh,
        in_specs=(whole, whole, line, line, P(("blk", "across"), None), P(("blk", "across"), None), line),
        out_specs=(whole, whole, whole, whole),
        check_vma=False,
    )
```

time: 224 us -> 96.4 us (0.43)
  the two profiles are of different devices: /device:TPU:0 before, /device:TPU:29 now
where the time goes in v1:
time: 96.4 us; the launch traced here: 96.5 us
  Pallas kernels  65.5 us (68%)
  waiting for transfers between devices  19.2 us (20%)
  starting transfers between devices  7.51 us (8%)
  other arithmetic  2.87 us (3%)
  between operations  1.4 us (1%)
    pallas_call x1, Pallas kernels, pair_sums(): pl.pallas_call(functools.partial(pair_kernel, count), out_shape=jax.Shape...  65.5 us
    ppermute x6, waiting for transfers between devices, passed_along(): return lax.ppermute(value, axis, pairs)  19.2 us
    ppermute x6, starting transfers between devices, passed_along(): return lax.ppermute(value, axis, pairs)  7.51 us
  transfers between devices with their start and end apart: 6, of which 4 were waited for; matrix products, arithmetic and copies ran while one was open for 0% of the time, Pallas kernels for 0%

profile of v1, /device:TPU:29, one launch (start us, length us, event | category | flops | bytes accessed | tf_op | source)
XLA Modules:
  0.0 96.5 jit_solution(16743120327465934756)
XLA Ops:
  0.6 0.0 copy-start.4
  0.6 0.7 convert_bitcast_fusion
  1.4 0.0 copy-done.4
  1.4 0.1 pad.3.clone
  1.5 0.0 copy-start.2
  1.5 1.0 %broadcast_multiply_fusion = f32[3,8192]{1,0:T(4,128)S(1)} fusion(f32[3,8192]{1,0:T(4,128)} %param.8, f32[8192]{0:T(1024)S(1)} %convert_bitcast_fusion), kind=kLoop, calls=%fused_computation.9 | loop fusion | flops 24576 | bytes 229376 | tf_op jit(solution)/shard_map/mul | solution.py:233
  2.5 0.0 copy-done.2
  2.5 0.1 pad_maximum_fusion.1.refs_2_
  2.6 1.3 %collective-permute-start.4 = (f32[8,8192]{1,0:T(8,128)S(1)}, f32[8,8192]{1,0:T(8,128)S(1)}, u32[]{:S(2)}, u32[]{:S(2)}) collective-permute-start(f32[8,8192]{1,0:T(8,128)S(1)} %pad_maximum_fusion.1.refs_2_), channel_id=1, source_target_pairs={{0,1},{1,0},{2,3},{3,2},{4,5},{5,4},{6,7},{7,6},{8,9},{9,8},{10,11... | collective-permute-start | bytes 786440 | tf_op jit(solution)/shard_map/ppermute | solution.py:22
  3.9 0.2 collective-permute-start.3
  4.1 1.2 %collective-permute-start.2 = (f32[8,8192]{1,0:T(8,128)S(1)}, f32[8,8192]{1,0:T(8,128)S(1)}, u32[]{:S(2)}, u32[]{:S(2)}) collective-permute-start(f32[8,8192]{1,0:T(8,128)S(1)} %pad_maximum_fusion.1.refs_2_), channel_id=1, source_target_pairs={{0,30},{2,0},{4,2},{6,4},{8,6},{10,8},{12,10},{14,12},{16,14},{18,... | collective-permute-start | bytes 786440 | tf_op jit(solution)/shard_map/ppermute | solution.py:22
  5.3 3.8 %collective-permute-start.1 = (f32[8,8192]{1,0:T(8,128)S(1)}, f32[8,8192]{1,0:T(8,128)S(1)}, u32[]{:S(2)}, u32[]{:S(2)}) collective-permute-start(f32[8,8192]{1,0:T(8,128)S(1)} %pad_maximum_fusion.1.refs_2_), channel_id=1, source_target_pairs={{0,2},{2,4},{4,6},{6,8},{8,10},{10,12},{12,14},{14,16},{16,18},{18... | collective-permute-start | bytes 786440 | tf_op jit(solution)/shard_map/ppermute | solution.py:22
  9.2 0.6 collective-permute-start
  10.5 0.0 collective-permute-done.4
  10.5 0.0 copy-start
  10.5 0.0 copy-start.1
  10.6 6.6 %collective-permute-done.3.refs_4_ = f32[8,8192]{1,0:T(8,128)S(1)} collective-permute-done((f32[8,8192]{1,0:T(8,128)S(1)}, f32[8,8192]{1,0:T(8,128)S(1)}, u32[]{:S(2)}, u32[]{:S(2)}) %collective-permute-start.3) | collective-permute-done | bytes 262176 | tf_op jit(solution)/shard_map/ppermute | solution.py:22
  17.2 0.3 collective-permute-done.2.refs_3_
  17.5 0.0 collective-permute-done.1.refs_1_
  17.5 7.3 %collective-permute-done.refs_0_ = f32[8,8192]{1,0:T(8,128)S(1)} collective-permute-done((f32[8,8192]{1,0:T(8,128)S(1)}, f32[8,8192]{1,0:T(8,128)S(1)}, u32[]{:S(2)}, u32[]{:S(2)}) %collective-permute-start) | collective-permute-done | bytes 262176 | tf_op jit(solution)/shard_map/ppermute | solution.py:22
  24.8 0.0 copy-done
  24.8 0.0 copy-done.1
  24.8 65.5 %pair_sums.1 = f32[8,16384]{1,0:T(8,128)S(1)} custom-call(s32[1]{0:T(128)S(6)} %copy.11.number, s32[1,256]{1,0:T(1,128)S(1)} %copy-done, s32[1,256]{1,0:T(1,128)S(1)} %copy-done.1, f32[8,8192]{1,0:T(8,128)S(1)} %collective-permute-done.refs_0_, f32[8,8192]{1,0:T(8,128)S(1)} %collective-permute-done.1.refs_1_, f32[8,8192]{1,0:T(8,128)S(1)} %pad_maximum_fusion.1.refs_2_, ...), custom_call_target="tpu_custom_call" | custom-call | tf_op jit(solution)/shard_map/pair_sums/pallas_call | solution.py:210
  90.3 0.0 copy-start.3
  90.3 0.3 collective-permute-start.5
  90.6 5.0 %collective-permute-done.5 = f32[8,8192]{1,0:T(8,128)S(1)} collective-permute-done((f32[8,8192]{1,0:T(8,128)S(1)}, f32[8,8192]{1,0:T(8,128)S(1)}, u32[]{:S(2)}, u32[]{:S(2)}) %collective-permute-start.5) | collective-permute-done | bytes 262176 | tf_op jit(solution)/shard_map/ppermute | solution.py:22
  95.6 0.0 copy-done.3
  95.6 0.9 multiply_add_fusion
  (6 shorter events, 0.2 us)
Async XLA Ops:
  0.6 0.8 copy-start.4
  1.5 1.0 %copy-start.2 = (f32[3,8192]{1,0:T(4,128)S(1)}, f32[3,8192]{1,0:T(4,128)}, u32[]{:S(2)}) copy-start(f32[3,8192]{1,0:T(4,128)} %param.7) | copy-start | bytes 294916
  2.6 7.9 %collective-permute-start.4 = (f32[8,8192]{1,0:T(8,128)S(1)}, f32[8,8192]{1,0:T(8,128)S(1)}, u32[]{:S(2)}, u32[]{:S(2)}) collective-permute-start(f32[8,8192]{1,0:T(8,128)S(1)} %pad_maximum_fusion.1.refs_2_), channel_id=1, source_target_pairs={{0,1},{1,0},{2,3},{3,2},{4,5},{5,4},{6,7},{7,6},{8,9},{9,8},{10,11... | collective-permute-start | bytes 786440 | tf_op jit(solution)/shard_map/ppermute | solution.py:22
  3.9 13.3 %collective-permute-start.3 = (f32[8,8192]{1,0:T(8,128)S(1)}, f32[8,8192]{1,0:T(8,128)S(1)}, u32[]{:S(2)}, u32[]{:S(2)}) collective-permute-start(f32[8,8192]{1,0:T(8,128)S(1)} %pad_maximum_fusion.1.refs_2_), channel_id=1, source_target_pairs={{0,28},{2,30},{4,0},{6,2},{8,4},{10,6},{12,8},{14,10},{16,12},{18,... | collective-permute-start | bytes 786440 | tf_op jit(solution)/shard_map/ppermute | solution.py:22
  4.1 13.4 %collective-permute-start.2 = (f32[8,8192]{1,0:T(8,128)S(1)}, f32[8,8192]{1,0:T(8,128)S(1)}, u32[]{:S(2)}, u32[]{:S(2)}) collective-permute-start(f32[8,8192]{1,0:T(8,128)S(1)} %pad_maximum_fusion.1.refs_2_), channel_id=1, source_target_pairs={{0,30},{2,0},{4,2},{6,4},{8,6},{10,8},{12,10},{14,12},{16,14},{18,... | collective-permute-start | bytes 786440 | tf_op jit(solution)/shard_map/ppermute | solution.py:22
  5.3 12.2 %collective-permute-start.1 = (f32[8,8192]{1,0:T(8,128)S(1)}, f32[8,8192]{1,0:T(8,128)S(1)}, u32[]{:S(2)}, u32[]{:S(2)}) collective-permute-start(f32[8,8192]{1,0:T(8,128)S(1)} %pad_maximum_fusion.1.refs_2_), channel_id=1, source_target_pairs={{0,2},{2,4},{4,6},{6,8},{8,10},{10,12},{12,14},{14,16},{16,18},{18... | collective-permute-start | bytes 786440 | tf_op jit(solution)/shard_map/ppermute | solution.py:22
  9.2 15.6 %collective-permute-start = (f32[8,8192]{1,0:T(8,128)S(1)}, f32[8,8192]{1,0:T(8,128)S(1)}, u32[]{:S(2)}, u32[]{:S(2)}) collective-permute-start(f32[8,8192]{1,0:T(8,128)S(1)} %pad_maximum_fusion.1.refs_2_), channel_id=1, source_target_pairs={{0,4},{2,6},{4,8},{6,10},{8,12},{10,14},{12,16},{14,18},{16,20},{1... | collective-permute-start | bytes 786440 | tf_op jit(solution)/shard_map/ppermute | solution.py:22
  10.5 14.3 %copy-start = (s32[1,256]{1,0:T(1,128)S(1)}, s32[1,256]{1,0:T(1,128)}, u32[]{:S(2)}) copy-start(s32[1,256]{1,0:T(1,128)} %target_list.1) | copy-start | bytes 3076
  10.5 14.3 %copy-start.1 = (s32[1,256]{1,0:T(1,128)S(1)}, s32[1,256]{1,0:T(1,128)}, u32[]{:S(2)}) copy-start(s32[1,256]{1,0:T(1,128)} %slot_list.1) | copy-start | bytes 3076
  90.3 5.3 %copy-start.3 = (f32[3,8192]{1,0:T(4,128)S(1)}, f32[3,8192]{1,0:T(4,128)}, u32[]{:S(2)}) copy-start(f32[3,8192]{1,0:T(4,128)} %param.8) | copy-start | bytes 294916
  90.3 5.3 %collective-permute-start.5 = (f32[8,8192]{1,0:T(8,128)S(1)}, f32[8,8192]{1,0:T(8,128)S(1)}, u32[]{:S(2)}, u32[]{:S(2)}) collective-permute-start(f32[8,8192]{1,0:T(8,128)S(1)} %slice_select_fusion), channel_id=1, source_target_pairs={{0,1},{1,0},{2,3},{3,2},{4,5},{5,4},{6,7},{7,6},{8,9},{9,8},{10,11... | collective-permute-start | bytes 786440 | tf_op jit(solution)/shard_map/ppermute | solution.py:22

commit v2 on v1

v2 whole, which is shorter than its diff:
```python
import jax
import jax.numpy as jnp
from jax import lax
from jax.experimental import pallas as pl
from jax.experimental.pallas import tpu as pltpu
from jax.sharding import PartitionSpec as P

BLOCK = 128
ROWS = 8
REACH = 2
GROUP = 8
FEATURES = 64

biot_factor = 0.07957747154594767
section_step = 0.05


def passed_along(value, axis, steps):
    count = lax.axis_size(axis)
    pairs = [(source, (source + steps) % count) for source in range(count)]
    return lax.ppermute(value, axis, pairs)


def rounded(value):
    return value.astype(jnp.bfloat16).astype(jnp.float32)


def split_three(value):
    first = rounded(value)
    rest = value - first
    second = rounded(rest)
    return first, second, rest - second


def cross(left, right):
    return [
        left[1] * right[2] - left[2] * right[1],
        left[2] * right[0] - left[0] * right[2],
        left[0] * right[1] - left[1] * right[0],
    ]


def tile_rows(index, rows):
    return pl.ds(pl.multiple_of(index * rows, rows), rows)


def component(ref, base, number, stride):
    return ref[pl.ds(base + number, GROUP, stride=stride), :]


def store_component(ref, base, number, stride, value):
    ref[pl.ds(base + number, GROUP, stride=stride), :] = value


def target_features(targets, step, centres, rows):
    base = pl.multiple_of(step * (GROUP * ROWS), GROUP * ROWS)
    pos = [component(targets, base, k, ROWS) for k in range(3)]
    strength = [component(targets, base, 5 + k, ROWS) for k in range(3)]
    for k in range(3):
        centre = jnp.broadcast_to(jnp.mean(pos[k], axis=1, keepdims=True), (GROUP, BLOCK))
        store_component(centres, base, k, ROWS, centre)
        pos[k] = pos[k] - centre
    norm = pos[0] * pos[0] + pos[1] * pos[1] + pos[2] * pos[2]
    own = pos[0] * strength[0] + pos[1] * strength[1] + pos[2] * strength[2]
    near = pos + [norm, jnp.ones_like(norm)]
    tilt = [0.5 * s for s in strength] + [own]
    for start, values in ((0, near), (32, tilt)):
        for k, value in enumerate(values):
            parts = split_three(value)
            for slot, part in enumerate((0, 1, 2, 0, 1, 0)):
                store_component(rows, 0, start + 5 * slot + k, FEATURES, parts[part])


def source_features(gathered, weight, left, charge):
    pos = [component(gathered, 0, k, ROWS) for k in range(3)]
    inv_core = component(gathered, 0, 4, ROWS)
    strength = [component(gathered, 0, 5 + k, ROWS) for k in range(3)]
    inv_square = inv_core * inv_core
    norm = pos[0] * pos[0] + pos[1] * pos[1] + pos[2] * pos[2]
    twice = -2.0 * inv_square
    shape = [p * twice for p in pos] + [inv_square, norm * inv_square + 1.0]
    for k, value in enumerate(shape):
        parts = split_three(value)
        for slot, part in enumerate((0, 0, 0, 1, 1, 2)):
            store_component(left, 0, 5 * slot + k, 32, parts[part])
    scale = inv_square * inv_core * weight
    for k, value in enumerate(strength + cross(pos, strength)):
        value = value * scale
        high = rounded(value)
        store_component(charge, 0, k, 2 * ROWS, high)
        store_component(charge, 0, ROWS + k, 2 * ROWS, value - high)


NT = (((1,), (1,)), ((), ()))


def pair_kernel(number, target_list, slot_list, *refs):
    count = 2 * REACH + 1
    windows, (targets_in, eye_ref) = refs[:count], refs[count : count + 2]
    (
        out_ref,
        window,
        targets,
        features,
        centres,
        total,
        feature_rows,
        gathered,
        left,
        charge,
        sems,
    ) = refs[count + 2 :]
    shard_rows = windows[0].shape[0]
    target_blocks = targets_in.shape[0] // ROWS
    list_length = target_list.shape[1]
    copies = [pltpu.make_async_copy(targets_in, targets, sems.at[count])]
    for k in range(count):
        copies.append(
            pltpu.make_async_copy(
                windows[k], window.at[pl.ds(k * shard_rows, shard_rows), :], sems.at[k]
            )
        )
    for copy in copies:
        copy.start()
    centres[...] = jnp.zeros_like(centres)
    feature_rows[...] = jnp.zeros_like(feature_rows)
    left[...] = jnp.zeros_like(left)
    charge[...] = jnp.zeros_like(charge)
    copies[0].wait()

    def prepare(step, carry):
        target_features(targets, step, centres, feature_rows)
        for u in range(GROUP):
            b = step * GROUP + u
            rows = feature_rows[u * FEATURES : (u + 1) * FEATURES, :].astype(jnp.bfloat16)
            turned = lax.dot_general(eye_ref[...], rows, NT, preferred_element_type=jnp.float32)
            features[b] = turned.astype(jnp.bfloat16)
            total[tile_rows(b, 2 * ROWS), :] = jnp.zeros((2 * ROWS, BLOCK), jnp.float32)
        return carry

    lax.fori_loop(0, target_blocks // GROUP, prepare, 0)
    for copy in copies[1:]:
        copy.wait()
    listed = number[0]

    def entry_at(step, u):
        return jnp.minimum(step * GROUP + u, list_length - 1)

    def prepare_sources(step):
        for u in range(GROUP):
            entry = entry_at(step, u)
            t = target_list[0, entry]
            s = slot_list[0, entry]
            gathered[u * ROWS : (u + 1) * ROWS, :] = (
                window[tile_rows(s, ROWS), :] - centres[tile_rows(t, ROWS), :]
            )
        order = lax.broadcasted_iota(jnp.int32, (GROUP, BLOCK), 0) + step * GROUP
        weight = jnp.where(order < listed, 1.0, 0.0).astype(jnp.float32)
        source_features(gathered, weight, left, charge)

    def matrices(step, u):
        t = target_list[0, entry_at(step, u)]
        shape = left[u * 32 : (u + 1) * 32, :].astype(jnp.bfloat16)
        blank = jnp.zeros_like(shape)
        shape = jnp.concatenate(
            [jnp.concatenate([shape, blank], axis=1), jnp.concatenate([blank, shape], axis=1)],
            axis=0,
        )
        return jnp.dot(features[t], shape, preferred_element_type=jnp.float32)

    def weights(both):
        near, tilt = both[:, :BLOCK], both[:, BLOCK:]
        q = lax.rsqrt(near)
        q2 = q * q
        q3 = q2 * q
        f = q3 * (q2 + (2.0 / 3.0))
        h = (q3 * q2) * (q2 + 0.4) * tilt
        fh = f.astype(jnp.bfloat16)
        fl = (f - fh.astype(jnp.float32)).astype(jnp.bfloat16)
        hh = h.astype(jnp.bfloat16)
        hl = (h - hh.astype(jnp.float32)).astype(jnp.bfloat16)
        return jnp.concatenate([fh, fl, hh, hl], axis=0)

    def add_up(step, u, stacked):
        t = target_list[0, entry_at(step, u)]
        pair = charge[u * 2 * ROWS : (u + 1) * 2 * ROWS, :].astype(jnp.bfloat16)
        sums = lax.dot_general(pair, stacked, NT, preferred_element_type=jnp.float32)
        fsum = sums[0:8, 0:128] + sums[8:16, 0:128] + sums[0:8, 128:256]
        hsum = sums[0:8, 256:384] + sums[8:16, 256:384] + sums[0:8, 384:512]
        total[tile_rows(t, 2 * ROWS), :] += jnp.concatenate([fsum, hsum], axis=0)

    steps = (listed + GROUP - 1) // GROUP
    prepare_sources(0)

    def turn(step, carry):
        both = [matrices(step, 0), matrices(step, 1)]
        stacked = []
        for u in range(GROUP):
            stacked.append(weights(both[u]))
            if u + 2 < GROUP:
                both.append(matrices(step, u + 2))
            if u >= 1:
                add_up(step, u - 1, stacked[u - 1])
        add_up(step, GROUP - 1, stacked[GROUP - 1])
        prepare_sources(step + 1)
        return carry

    lax.fori_loop(0, steps, turn, 0)

    def finish(step, carry):
        base = pl.multiple_of(step * (GROUP * ROWS), GROUP * ROWS)
        wide = pl.multiple_of(step * (GROUP * 2 * ROWS), GROUP * 2 * ROWS)
        pos = [
            component(targets, base, k, ROWS) - component(centres, base, k, ROWS) for k in range(3)
        ]
        strength = [component(targets, base, 5 + k, ROWS) for k in range(3)]
        fa, fb, ha, hb = [
            [component(total, wide, start + k, 2 * ROWS) for k in range(3)] for start in (0, 3, 8, 11)
        ]
        swirl = cross(pos, fa)
        lean = cross(strength, fa)
        bend = cross(pos, ha)
        for k in range(3):
            velocity = (-1.5 * biot_factor) * (swirl[k] - fb[k])
            stretch = (-1.5 * biot_factor) * lean[k] + (7.5 * biot_factor) * (bend[k] - hb[k])
            store_component(out_ref, base, k, ROWS, velocity)
            store_component(out_ref, base, 3 + k, ROWS, stretch)
        for k in (6, 7):
            store_component(out_ref, base, k, ROWS, jnp.zeros_like(pos[0]))
        return carry

    lax.fori_loop(0, target_blocks // GROUP, finish, 0)


def pair_sums(number, target_list, slot_list, windows, targets):
    count = len(windows)
    shard_rows = windows[0].shape[0]
    target_rows = targets.shape[0]
    target_blocks = target_rows // ROWS
    eye = jnp.eye(BLOCK, dtype=jnp.bfloat16)
    smem = pl.BlockSpec(memory_space=pltpu.SMEM)
    anyspace = pl.BlockSpec(memory_space=pl.ANY)
    vmem = pl.BlockSpec(memory_space=pltpu.VMEM)
    return pl.pallas_call(
        pair_kernel,
        out_shape=jax.ShapeDtypeStruct((target_rows, BLOCK), jnp.float32),
        in_specs=[smem] * 3 + [anyspace] * (count + 1) + [vmem],
        out_specs=vmem,
        scratch_shapes=[
            pltpu.VMEM((count * shard_rows, BLOCK), jnp.float32),
            pltpu.VMEM((target_rows, BLOCK), jnp.float32),
            pltpu.VMEM((target_blocks, BLOCK, FEATURES), jnp.bfloat16),
            pltpu.VMEM((target_rows, BLOCK), jnp.float32),
            pltpu.VMEM((2 * target_rows, BLOCK), jnp.float32),
            pltpu.VMEM((GROUP * FEATURES, BLOCK), jnp.float32),
            pltpu.VMEM((GROUP * ROWS, BLOCK), jnp.float32),
            pltpu.VMEM((GROUP * 32, BLOCK), jnp.float32),
            pltpu.VMEM((GROUP * 2 * ROWS, BLOCK), jnp.float32),
            pltpu.SemaphoreType.DMA((count + 1,)),
        ],
        compiler_params=pltpu.CompilerParams(vmem_limit_bytes=48 * 1024 * 1024),
        name="pair_sums",
    )(number, target_list, slot_list, *windows, targets, eye)


def tiles(value, blocks):
    rows = value.shape[0]
    return value.reshape(rows, blocks, BLOCK).transpose(1, 0, 2).reshape(blocks * rows, BLOCK)


def rows_again(value, blocks):
    rows = value.shape[0] // blocks
    return value.reshape(blocks, rows, BLOCK).transpose(1, 0, 2).reshape(rows, blocks * BLOCK)


def shards(positions, strengths, radius, block_count, pair_target, pair_slot, pair_count):
    blocks = block_count.shape[0]
    lanes = blocks * BLOCK
    slot_index = jnp.arange(BLOCK, dtype=jnp.int32)
    alive = (slot_index[None, :] < block_count[:, None]).astype(jnp.float32)
    live_strengths = strengths * alive.reshape(1, lanes)
    resident = jnp.concatenate(
        [positions, jnp.ones((1, lanes), jnp.float32), 1.0 / radius[None, :], live_strengths], axis=0
    )
    resident = tiles(resident, blocks)
    windows = [
        resident if away == 0 else passed_along(resident, "blk", -away)
        for away in range(-REACH, REACH + 1)
    ]
    members = lax.axis_size("across")
    me = lax.axis_index("across")
    if members == 2:
        other = passed_along(resident, "across", 1)
        first = jnp.where(me == 0, resident, other)
        second = jnp.where(me == 0, other, resident)
        targets = jnp.concatenate([first, second], axis=0)
    else:
        targets = lax.all_gather(resident, "across", axis=0, tiled=True)
    sums = pair_sums(pair_count, pair_target, pair_slot, windows, targets)
    if members == 2:
        first, second = sums[: blocks * ROWS], sums[blocks * ROWS :]
        mine = jnp.where(me == 0, first, second)
        away = jnp.where(me == 0, second, first)
        result = mine + passed_along(away, "across", 1)
    else:
        result = lax.psum_scatter(sums, "across", scatter_dimension=0, tiled=True)
    result = rows_again(result, blocks)
    velocity = result[0:3]
    stretching = result[3:6]
    return (
        velocity,
        stretching,
        positions + section_step * velocity,
        live_strengths + section_step * stretching,
    )


def solution(mesh):
    whole = P(None, ("blk", "across"))
    line = P(("blk", "across"))
    return jax.shard_map(
        shards,
        mesh=mesh,
        in_specs=(whole, whole, line, line, P(("blk", "across"), None), P(("blk", "across"), None), line),
        out_specs=(whole, whole, whole, whole),
        check_vma=False,
    )
```

time: 96.4 us -> 58.9 us (0.61)
  Pallas kernels: 65.5 us -> 27.9 us
    pallas_call x1, Pallas kernels: 65.5 us -> 27.9 us  [pair_sums(): pl.pallas_call(pair_kernel, out_shape=jax.ShapeDtypeStruct((target_rows,...]
    mul x1 -> x0, other arithmetic: 0.97 us -> none  [shards(): live_strengths = strengths * alive.reshape(1, lanes)]
where the time goes in v2:
time: 58.9 us; the launch traced here: 59 us
  Pallas kernels  27.9 us (47%)
  waiting for transfers between devices  19.2 us (33%)
  starting transfers between devices  7.51 us (13%)
  other arithmetic  2.87 us (5%)
  between operations  1.4 us (2%)
    pallas_call x1, Pallas kernels, pair_sums(): pl.pallas_call(pair_kernel, out_shape=jax.ShapeDtypeStruct((target_rows,...  27.9 us
    ppermute x6, waiting for transfers between devices, passed_along(): return lax.ppermute(value, axis, pairs)  19.2 us
    ppermute x6, starting transfers between devices, passed_along(): return lax.ppermute(value, axis, pairs)  7.51 us
  transfers between devices with their start and end apart: 6, of which 4 were waited for; matrix products, arithmetic and copies ran while one was open for 0% of the time, Pallas kernels for 0%

profile of v2, /device:TPU:29, one launch (start us, length us, event | category | flops | bytes accessed | tf_op | source)
XLA Modules:
  0.0 59.0 jit_solution(16548191464310787090)
XLA Ops:
  0.6 0.0 copy-start.4
  0.6 0.7 %convert_bitcast_fusion = f32[8192]{0:T(1024)S(1)} fusion(s32[64]{0:T(128)} %param.10), kind=kLoop, calls=%fused_computation.13 | loop fusion | flops 16384 | bytes 33024 | tf_op jit(solution)/shard_map/convert_element_type | solution.py:280
  1.4 0.0 copy-done.4
  1.4 0.1 pad.3.clone
  1.5 0.0 copy-start.2
  1.5 1.0 %multiply_bitcast_fusion = f32[3,64,128]{2,0,1:T(4,128)S(1)} fusion(f32[3,8192]{1,0:T(4,128)} %param.8, f32[8192]{0:T(1024)S(1)} %convert_bitcast_fusion), kind=kLoop, calls=%fused_computation.10 | loop fusion | flops 24576 | bytes 229376 | tf_op jit(solution)/shard_map/concatenate | solution.py:282
  2.5 0.0 copy-done.2
  2.5 0.1 maximum_bitcast_fusion.refs_2_
  2.6 1.3 %collective-permute-start.4 = (f32[512,128]{1,0:T(8,128)S(1)}, f32[512,128]{1,0:T(8,128)S(1)}, u32[]{:S(2)}, u32[]{:S(2)}) collective-permute-start(f32[512,128]{1,0:T(8,128)S(1)} %maximum_bitcast_fusion.refs_2_), channel_id=1, source_target_pairs={{0,1},{1,0},{2,3},{3,2},{4,5},{5,4},{6,7},{7,6},{8,9},{9,8},{10,11... | collective-permute-start | bytes 786440 | tf_op jit(solution)/shard_map/ppermute | solution.py:21
  3.9 0.2 collective-permute-start.3
  4.1 1.2 %collective-permute-start.2 = (f32[512,128]{1,0:T(8,128)S(1)}, f32[512,128]{1,0:T(8,128)S(1)}, u32[]{:S(2)}, u32[]{:S(2)}) collective-permute-start(f32[512,128]{1,0:T(8,128)S(1)} %maximum_bitcast_fusion.refs_2_), channel_id=1, source_target_pairs={{0,30},{2,0},{4,2},{6,4},{8,6},{10,8},{12,10},{14,12},{16,14},{18,... | collective-permute-start | bytes 786440 | tf_op jit(solution)/shard_map/ppermute | solution.py:21
  5.3 3.8 %collective-permute-start.1 = (f32[512,128]{1,0:T(8,128)S(1)}, f32[512,128]{1,0:T(8,128)S(1)}, u32[]{:S(2)}, u32[]{:S(2)}) collective-permute-start(f32[512,128]{1,0:T(8,128)S(1)} %maximum_bitcast_fusion.refs_2_), channel_id=1, source_target_pairs={{0,2},{2,4},{4,6},{6,8},{8,10},{10,12},{12,14},{14,16},{16,18},{18... | collective-permute-start | bytes 786440 | tf_op jit(solution)/shard_map/ppermute | solution.py:21
  9.2 0.6 %collective-permute-start = (f32[512,128]{1,0:T(8,128)S(1)}, f32[512,128]{1,0:T(8,128)S(1)}, u32[]{:S(2)}, u32[]{:S(2)}) collective-permute-start(f32[512,128]{1,0:T(8,128)S(1)} %maximum_bitcast_fusion.refs_2_), channel_id=1, source_target_pairs={{0,4},{2,6},{4,8},{6,10},{8,12},{10,14},{12,16},{14,18},{16,20},{1... | collective-permute-start | bytes 786440 | tf_op jit(solution)/shard_map/ppermute | solution.py:21
  10.5 0.0 collective-permute-done.4
  10.5 0.0 copy-start
  10.5 0.0 copy-start.1
  10.6 6.6 %collective-permute-done.3.refs_4_ = f32[512,128]{1,0:T(8,128)S(1)} collective-permute-done((f32[512,128]{1,0:T(8,128)S(1)}, f32[512,128]{1,0:T(8,128)S(1)}, u32[]{:S(2)}, u32[]{:S(2)}) %collective-permute-start.3) | collective-permute-done | bytes 262176 | tf_op jit(solution)/shard_map/ppermute | solution.py:21
  17.2 0.3 collective-permute-done.2.refs_3_
  17.5 0.0 collective-permute-done.1.refs_1_
  17.5 7.3 %collective-permute-done.refs_0_ = f32[512,128]{1,0:T(8,128)S(1)} collective-permute-done((f32[512,128]{1,0:T(8,128)S(1)}, f32[512,128]{1,0:T(8,128)S(1)}, u32[]{:S(2)}, u32[]{:S(2)}) %collective-permute-start) | collective-permute-done | bytes 262176 | tf_op jit(solution)/shard_map/ppermute | solution.py:21
  24.8 0.0 copy-done
  24.8 0.0 copy-done.1
  24.8 27.9 %pair_sums.1 = f32[1024,128]{1,0:T(8,128)S(1)} custom-call(s32[1]{0:T(128)S(6)} %copy.15.number, s32[1,256]{1,0:T(1,128)S(1)} %copy-done, s32[1,256]{1,0:T(1,128)S(1)} %copy-done.1, f32[512,128]{1,0:T(8,128)S(1)} %collective-permute-done.refs_0_, f32[512,128]{1,0:T(8,128)S(1)} %collective-permute-done.1.refs_1_, f32[512,128]{1,0:T(8,128)S(1)} %maximum_bitcast_fusion.refs_2_, ...), custom_call_target="tpu_custom_call" | custom-call | tf_op jit(solution)/shard_map/pair_sums/pallas_call | solution.py:244
  52.7 0.0 copy-start.3
  52.7 0.3 collective-permute-start.5
  53.1 5.0 %collective-permute-done.5 = f32[512,128]{1,0:T(8,128)S(1)} collective-permute-done((f32[512,128]{1,0:T(8,128)S(1)}, f32[512,128]{1,0:T(8,128)S(1)}, u32[]{:S(2)}, u32[]{:S(2)}) %collective-permute-start.5) | collective-permute-done | bytes 262176 | tf_op jit(solution)/shard_map/ppermute | solution.py:21
  58.1 0.0 copy-done.3
  58.1 0.9 %multiply_add_fusion = (f32[3,8192]{1,0:T(4,128)}, f32[3,8192]{1,0:T(4,128)}, f32[3,8192]{1,0:T(4,128)}, f32[3,8192]{1,0:T(4,128)}) fusion(f32[3,8192]{1,0:T(4,128)S(1)} %copy-done.3, f32[8192]{0:T(1024)S(1)} %convert_bitcast_fusion, f32[8,64,128]{2,0,1:T(8,128)S(1)} %add_bitcast_fusion, f32[3,8192]{1,0:T(4,128)S(1)} %copy-done.2), kind=kLoop, calls=%fused_computation.6 | loop fusion | flops 122880 | bytes 819200 | tf_op jit(solution)/shard_map/add | solution.py:314
  (6 shorter events, 0.2 us)
Async XLA Ops:
  0.6 0.8 %copy-start.4 = (f32[8192]{0:T(1024)S(1)}, f32[8192]{0:T(1024)}, u32[]{:S(2)}) copy-start(f32[8192]{0:T(1024)} %param.9) | copy-start | bytes 98308
  1.5 1.0 %copy-start.2 = (f32[3,8192]{1,0:T(4,128)S(1)}, f32[3,8192]{1,0:T(4,128)}, u32[]{:S(2)}) copy-start(f32[3,8192]{1,0:T(4,128)} %param.7) | copy-start | bytes 294916
  2.6 7.9 %collective-permute-start.4 = (f32[512,128]{1,0:T(8,128)S(1)}, f32[512,128]{1,0:T(8,128)S(1)}, u32[]{:S(2)}, u32[]{:S(2)}) collective-permute-start(f32[512,128]{1,0:T(8,128)S(1)} %maximum_bitcast_fusion.refs_2_), channel_id=1, source_target_pairs={{0,1},{1,0},{2,3},{3,2},{4,5},{5,4},{6,7},{7,6},{8,9},{9,8},{10,11... | collective-permute-start | bytes 786440 | tf_op jit(solution)/shard_map/ppermute | solution.py:21
  3.9 13.3 %collective-permute-start.3 = (f32[512,128]{1,0:T(8,128)S(1)}, f32[512,128]{1,0:T(8,128)S(1)}, u32[]{:S(2)}, u32[]{:S(2)}) collective-permute-start(f32[512,128]{1,0:T(8,128)S(1)} %maximum_bitcast_fusion.refs_2_), channel_id=1, source_target_pairs={{0,28},{2,30},{4,0},{6,2},{8,4},{10,6},{12,8},{14,10},{16,12},{18,... | collective-permute-start | bytes 786440 | tf_op jit(solution)/shard_map/ppermute | solution.py:21
  4.1 13.4 %collective-permute-start.2 = (f32[512,128]{1,0:T(8,128)S(1)}, f32[512,128]{1,0:T(8,128)S(1)}, u32[]{:S(2)}, u32[]{:S(2)}) collective-permute-start(f32[512,128]{1,0:T(8,128)S(1)} %maximum_bitcast_fusion.refs_2_), channel_id=1, source_target_pairs={{0,30},{2,0},{4,2},{6,4},{8,6},{10,8},{12,10},{14,12},{16,14},{18,... | collective-permute-start | bytes 786440 | tf_op jit(solution)/shard_map/ppermute | solution.py:21
  5.3 12.2 %collective-permute-start.1 = (f32[512,128]{1,0:T(8,128)S(1)}, f32[512,128]{1,0:T(8,128)S(1)}, u32[]{:S(2)}, u32[]{:S(2)}) collective-permute-start(f32[512,128]{1,0:T(8,128)S(1)} %maximum_bitcast_fusion.refs_2_), channel_id=1, source_target_pairs={{0,2},{2,4},{4,6},{6,8},{8,10},{10,12},{12,14},{14,16},{16,18},{18... | collective-permute-start | bytes 786440 | tf_op jit(solution)/shard_map/ppermute | solution.py:21
  9.2 15.6 %collective-permute-start = (f32[512,128]{1,0:T(8,128)S(1)}, f32[512,128]{1,0:T(8,128)S(1)}, u32[]{:S(2)}, u32[]{:S(2)}) collective-permute-start(f32[512,128]{1,0:T(8,128)S(1)} %maximum_bitcast_fusion.refs_2_), channel_id=1, source_target_pairs={{0,4},{2,6},{4,8},{6,10},{8,12},{10,14},{12,16},{14,18},{16,20},{1... | collective-permute-start | bytes 786440 | tf_op jit(solution)/shard_map/ppermute | solution.py:21
  10.5 14.3 %copy-start = (s32[1,256]{1,0:T(1,128)S(1)}, s32[1,256]{1,0:T(1,128)}, u32[]{:S(2)}) copy-start(s32[1,256]{1,0:T(1,128)} %target_list.1) | copy-start | bytes 3076
  10.5 14.3 %copy-start.1 = (s32[1,256]{1,0:T(1,128)S(1)}, s32[1,256]{1,0:T(1,128)}, u32[]{:S(2)}) copy-start(s32[1,256]{1,0:T(1,128)} %slot_list.1) | copy-start | bytes 3076
  52.7 5.3 %copy-start.3 = (f32[3,8192]{1,0:T(4,128)S(1)}, f32[3,8192]{1,0:T(4,128)}, u32[]{:S(2)}) copy-start(f32[3,8192]{1,0:T(4,128)} %param.8) | copy-start | bytes 294916
  52.7 5.3 %collective-permute-start.5 = (f32[512,128]{1,0:T(8,128)S(1)}, f32[512,128]{1,0:T(8,128)S(1)}, u32[]{:S(2)}, u32[]{:S(2)}) collective-permute-start(f32[512,128]{1,0:T(8,128)S(1)} %slice_select_fusion), channel_id=1, source_target_pairs={{0,1},{1,0},{2,3},{3,2},{4,5},{5,4},{6,7},{7,6},{8,9},{9,8},{10,11... | collective-permute-start | bytes 786440 | tf_op jit(solution)/shard_map/ppermute | solution.py:21

commit v3 on v2

v3 whole, which is shorter than its diff:
```python
import jax
import jax.numpy as jnp
from jax import lax
from jax.experimental import pallas as pl
from jax.experimental.pallas import tpu as pltpu
from jax.sharding import PartitionSpec as P

BLOCK = 128
ROWS = 8
SENT = 7
REACH = 2
GROUP = 8
FEATURES = 64
CLASSES = 4

biot_factor = 0.07957747154594767
section_step = 0.05


def moved(value, axis, target_of):
    pairs = [(source, target_of(source)) for source in range(lax.axis_size(axis))]
    return lax.ppermute(value, axis, pairs)


def to_other_core(source):
    return source ^ 1


def to_paired_chip(source):
    return source ^ 2


def along_chips(count):
    return lambda source: (source + (4 if source & 2 == 0 else -4)) % count


HOME_FLOPS = 10**10
NEAR_FLOPS = 10**10
FAR_FLOPS = 10**10


def rounded(value):
    return value.astype(jnp.bfloat16).astype(jnp.float32)


def split_three(value):
    first = rounded(value)
    rest = value - first
    second = rounded(rest)
    return first, second, rest - second


def cross(left, right):
    return [
        left[1] * right[2] - left[2] * right[1],
        left[2] * right[0] - left[0] * right[2],
        left[0] * right[1] - left[1] * right[0],
    ]


def tile_rows(index, rows):
    return pl.ds(pl.multiple_of(index * rows, rows), rows)


def component(ref, base, number, stride):
    return ref[pl.ds(base + number, GROUP, stride=stride), :]


def store_component(ref, base, number, stride, value):
    ref[pl.ds(base + number, GROUP, stride=stride), :] = value


def target_features(targets, step, centres, rows):
    base = pl.multiple_of(step * (GROUP * ROWS), GROUP * ROWS)
    pos = [component(targets, base, k, ROWS) for k in range(3)]
    strength = [component(targets, base, 3 + k, ROWS) for k in range(3)]
    for k in range(3):
        centre = jnp.broadcast_to(jnp.mean(pos[k], axis=1, keepdims=True), (GROUP, BLOCK))
        store_component(centres, base, k, ROWS, centre)
        pos[k] = pos[k] - centre
    for k in range(3, ROWS):
        store_component(centres, base, k, ROWS, jnp.zeros_like(pos[0]))
    norm = pos[0] * pos[0] + pos[1] * pos[1] + pos[2] * pos[2]
    own = pos[0] * strength[0] + pos[1] * strength[1] + pos[2] * strength[2]
    near = pos + [norm, jnp.ones_like(norm)]
    tilt = [0.5 * s for s in strength] + [own]
    for start, values in ((0, near), (32, tilt)):
        for k, value in enumerate(values):
            parts = split_three(value)
            for slot, part in enumerate((0, 1, 2, 0, 1, 0)):
                store_component(rows, 0, start + 5 * slot + k, FEATURES, parts[part])


def source_features(gathered, weight, left, charge):
    pos = [component(gathered, 0, k, ROWS) for k in range(3)]
    strength = [component(gathered, 0, 3 + k, ROWS) for k in range(3)]
    inv_core = component(gathered, 0, 6, ROWS)
    inv_square = inv_core * inv_core
    norm = pos[0] * pos[0] + pos[1] * pos[1] + pos[2] * pos[2]
    twice = -2.0 * inv_square
    shape = [p * twice for p in pos] + [inv_square, norm * inv_square + 1.0]
    for k, value in enumerate(shape):
        parts = split_three(value)
        for slot, part in enumerate((0, 0, 0, 1, 1, 2)):
            store_component(left, 0, 5 * slot + k, 32, parts[part])
    scale = inv_square * inv_core * weight
    for k, value in enumerate(strength + cross(pos, strength)):
        value = value * scale
        high = rounded(value)
        store_component(charge, 0, k, 2 * ROWS, high)
        store_component(charge, 0, ROWS + k, 2 * ROWS, value - high)


NT = (((1,), (1,)), ((), ()))


def unpack(sent, tile_ref, first):
    blocks = sent.shape[0] // SENT
    for j in range(blocks // GROUP):
        base = pl.multiple_of((first + j * GROUP) * ROWS, GROUP * ROWS)
        for k in range(SENT):
            rows = sent[k * blocks + j * GROUP : k * blocks + (j + 1) * GROUP, :]
            store_component(tile_ref, base, k, ROWS, rows)


def prepare_targets(first, last, state, eye, feature_rows):
    targets, features, centres, total = state

    def prepare(step, carry):
        target_features(targets, step, centres, feature_rows)
        for u in range(GROUP):
            b = step * GROUP + u
            rows = feature_rows[u * FEATURES : (u + 1) * FEATURES, :].astype(jnp.bfloat16)
            turned = lax.dot_general(eye, rows, NT, preferred_element_type=jnp.float32)
            features[b] = turned.astype(jnp.bfloat16)
            total[tile_rows(b, 2 * ROWS), :] = jnp.zeros((2 * ROWS, BLOCK), jnp.float32)
        return carry

    lax.fori_loop(first // GROUP, last // GROUP, prepare, 0)


def unit_matrix():
    row = lax.broadcasted_iota(jnp.int32, (BLOCK, BLOCK), 0)
    column = lax.broadcasted_iota(jnp.int32, (BLOCK, BLOCK), 1)
    return jnp.where(row == column, 1.0, 0.0).astype(jnp.bfloat16)


def run_class(kind, lists, window, state, scratch):
    target_list, slot_list, counts = lists
    _, features, centres, total = state
    gathered, left, charge = scratch
    length = target_list.shape[0] // (CLASSES + 1)
    listed = counts[kind]

    def entry_at(step, u):
        return kind * length + jnp.minimum(step * GROUP + u, listed - 1)

    def prepare_sources(step):
        for u in range(GROUP):
            entry = entry_at(step, u)
            gathered[u * ROWS : (u + 1) * ROWS, :] = (
                window[tile_rows(slot_list[entry], ROWS), :]
                - centres[tile_rows(target_list[entry], ROWS), :]
            )
        order = lax.broadcasted_iota(jnp.int32, (GROUP, BLOCK), 0) + step * GROUP
        weight = jnp.where(order < listed, 1.0, 0.0).astype(jnp.float32)
        source_features(gathered, weight, left, charge)

    def matrices(step, u):
        shape = left[u * 32 : (u + 1) * 32, :].astype(jnp.bfloat16)
        blank = jnp.zeros_like(shape)
        shape = jnp.concatenate(
            [jnp.concatenate([shape, blank], axis=1), jnp.concatenate([blank, shape], axis=1)],
            axis=0,
        )
        t = target_list[entry_at(step, u)]
        return jnp.dot(features[t], shape, preferred_element_type=jnp.float32)

    def weights(both):
        near, tilt = both[:, :BLOCK], both[:, BLOCK:]
        q = lax.rsqrt(near)
        q2 = q * q
        q3 = q2 * q
        f = q3 * (q2 + (2.0 / 3.0))
        h = (q3 * q2) * (q2 + 0.4) * tilt
        fh = f.astype(jnp.bfloat16)
        fl = (f - fh.astype(jnp.float32)).astype(jnp.bfloat16)
        hh = h.astype(jnp.bfloat16)
        hl = (h - hh.astype(jnp.float32)).astype(jnp.bfloat16)
        return jnp.concatenate([fh, fl, hh, hl], axis=0)

    def add_up(step, u, stacked):
        t = target_list[entry_at(step, u)]
        pair = charge[u * 2 * ROWS : (u + 1) * 2 * ROWS, :].astype(jnp.bfloat16)
        sums = lax.dot_general(pair, stacked, NT, preferred_element_type=jnp.float32)
        fsum = sums[0:8, 0:128] + sums[8:16, 0:128] + sums[0:8, 128:256]
        hsum = sums[0:8, 256:384] + sums[8:16, 256:384] + sums[0:8, 384:512]
        total[tile_rows(t, 2 * ROWS), :] += jnp.concatenate([fsum, hsum], axis=0)

    def turn(step, carry):
        both = [matrices(step, 0), matrices(step, 1)]
        stacked = []
        for u in range(GROUP):
            stacked.append(weights(both[u]))
            if u + 2 < GROUP:
                both.append(matrices(step, u + 2))
            if u >= 1:
                add_up(step, u - 1, stacked[u - 1])
        add_up(step, GROUP - 1, stacked[GROUP - 1])
        prepare_sources(step + 1)
        return carry

    @pl.when(listed > 0)
    def _():
        left[...] = jnp.zeros_like(left)
        charge[...] = jnp.zeros_like(charge)
        prepare_sources(0)
        lax.fori_loop(0, (listed + GROUP - 1) // GROUP, turn, 0)


def finish(first, last, state, out_ref):
    targets, _, centres, total = state
    blocks = out_ref.shape[1] // 6

    def one(step, carry):
        base = pl.multiple_of((first + step * GROUP) * ROWS, GROUP * ROWS)
        wide = pl.multiple_of((first + step * GROUP) * 2 * ROWS, GROUP * 2 * ROWS)
        pos = [
            component(targets, base, k, ROWS) - component(centres, base, k, ROWS) for k in range(3)
        ]
        strength = [component(targets, base, 3 + k, ROWS) for k in range(3)]
        fa, fb, ha, hb = [
            [component(total, wide, start + k, 2 * ROWS) for k in range(3)] for start in (0, 3, 8, 11)
        ]
        swirl = cross(pos, fa)
        lean = cross(strength, fa)
        bend = cross(pos, ha)
        member = step * GROUP // blocks
        inside = lax.rem(step * GROUP, blocks)
        for k in range(3):
            velocity = (-1.5 * biot_factor) * (swirl[k] - fb[k])
            stretch = (-1.5 * biot_factor) * lean[k] + (7.5 * biot_factor) * (bend[k] - hb[k])
            out_ref[member, pl.ds(pl.multiple_of(k * blocks + inside, GROUP), GROUP), :] = velocity
            out_ref[member, pl.ds(pl.multiple_of((3 + k) * blocks + inside, GROUP), GROUP), :] = stretch
        return carry

    lax.fori_loop(0, (last - first) // GROUP, one, 0)


def pack_kernel(block_count, positions, strengths, radius, sent):
    blocks = block_count.shape[0]
    lane = lax.broadcasted_iota(jnp.int32, (3, BLOCK), 1)
    for b in range(blocks):
        lanes = slice(b * BLOCK, (b + 1) * BLOCK)
        sent[pl.ds(b, 3, stride=blocks), :] = positions[:, lanes]
        live = jnp.where(lane < block_count[b], strengths[:, lanes], 0.0)
        sent[pl.ds(3 * blocks + b, 3, stride=blocks), :] = live
    sent[6 * blocks :, :] = 1.0 / radius[...]


def sort_list(number, pair_target, pair_slot, lists, blocks, members):
    target_list, slot_list, counts = lists
    length = pair_target.shape[1]
    listed = number[0]
    me = lax.axis_index("across")
    partner = jnp.where(lax.axis_index("blk") % 2 == 0, REACH + 1, REACH - 1)

    def one(step, carry):
        for u in range(GROUP):
            entry = jnp.minimum(step * GROUP + u, length - 1)
            t = pair_target[0, entry]
            s = pair_slot[0, entry]
            t = t - me * blocks
            t = jnp.where(t < 0, t + members * blocks, t)
            run = s // blocks
            mine = t < blocks
            home = run == REACH
            near = home | (run == partner)
            kind = jnp.where(near, jnp.where(home & mine, 0, 1), jnp.where(mine, 3, 2))
            kind = jnp.where(step * GROUP + u < listed, kind, CLASSES)
            at = kind * length
            for c in range(CLASSES):
                at = at + jnp.where(kind == c, carry[c], 0)
            target_list[at] = t
            slot_list[at] = s
            carry = tuple(carry[c] + jnp.where(kind == c, 1, 0) for c in range(CLASSES))
        return carry

    zero = jnp.int32(0)
    found = lax.fori_loop(0, (listed + GROUP - 1) // GROUP, one, (zero,) * CLASSES)
    for c in range(CLASSES):
        counts[c] = found[c]


def home_kernel(number, pair_target, pair_slot, own, *refs):
    target_list, slot_list, counts, targets, features, centres, total = refs[:7]
    feature_rows, gathered, left, charge = refs[7:]
    lists, state = refs[:3], refs[3:7]
    blocks = own.shape[0] // SENT
    unpack(own, targets, 0)
    feature_rows[...] = jnp.zeros_like(feature_rows)
    prepare_targets(0, blocks, state, unit_matrix(), feature_rows)
    sort_list(number, pair_target, pair_slot, lists, blocks, targets.shape[0] // ROWS // blocks)
    run_class(0, lists, targets_as_window(targets, blocks), state, (gathered, left, charge))


class targets_as_window:
    def __init__(self, targets, blocks):
        self.targets, self.start = targets, REACH * blocks * ROWS

    def __getitem__(self, index):
        rows, lanes = index
        return self.targets[pl.ds(pl.multiple_of(rows.start - self.start, ROWS), rows.size), lanes]


def near_kernel(*refs, members):
    target_list, slot_list, counts, own, partner = refs[:5]
    others = refs[5 : 5 + members - 1]
    given = refs[5 + members - 1 :][4:]
    targets, features, centres, total = state = given[:4]
    window, feature_rows, gathered, left, charge = given[4:]
    lists = refs[:3]
    blocks = own.shape[0] // SENT
    for r, other in enumerate(others):
        unpack(other, targets, (r + 1) * blocks)
    feature_rows[...] = jnp.zeros_like(feature_rows)
    prepare_targets(blocks, members * blocks, state, unit_matrix(), feature_rows)
    unpack(own, window, REACH * blocks)
    side = jnp.where(lax.axis_index("blk") % 2 == 0, REACH + 1, REACH - 1)
    unpack(partner, window, side * blocks)
    run_class(1, lists, window, state, (gathered, left, charge))


def far_kernel(target_list, slot_list, counts, paired, passed, crossed, *refs):
    given = refs[4:]
    targets, features, centres, total = state = given[:4]
    window, out_ref = given[4:6]
    gathered, left, charge = given[6:]
    lists = (target_list, slot_list, counts)
    blocks = paired.shape[0] // SENT
    shard = lax.axis_index("blk")
    even = shard // 2 % 2 == 0
    unpack(paired, window, jnp.where(even, 2 * REACH, 0) * blocks)
    unpack(passed, window, jnp.where(even, 0, 2 * REACH) * blocks)
    unpack(crossed, window, jnp.where(shard % 2 == 0, REACH - 1, REACH + 1) * blocks)
    run_class(2, lists, window, state, (gathered, left, charge))
    finish(blocks, targets.shape[0] // ROWS, state, out_ref)


def last_kernel(target_list, slot_list, counts, window, *refs):
    given = refs[4:]
    targets, features, centres, total = state = given[:4]
    out_ref, gathered, left, charge = given[4:]
    lists = (target_list, slot_list, counts)
    run_class(3, lists, window, state, (gathered, left, charge))
    finish(0, window.shape[0] // ROWS // (2 * REACH + 1), state, out_ref)


def section_kernel(sent, sums, *refs):
    returned, (velocity, stretching, section_positions, section_strengths) = refs[:-4], refs[-4:]
    blocks = sent.shape[0] // SENT

    for b in range(blocks):
        lanes = slice(b * BLOCK, (b + 1) * BLOCK)

        def rows(ref, start):
            return ref[pl.ds(start * blocks + b, 3, stride=blocks), :]

        for start, result, stepped in ((0, velocity, section_positions), (3, stretching, section_strengths)):
            value = rows(sums, start)
            for other in returned:
                value = value + rows(other, start)
            result[:, lanes] = value
            stepped[:, lanes] = rows(sent, start) + section_step * value


def call(kernel, name, inputs, outputs, scratch, aliases=None, flops=0):
    smem = pl.BlockSpec(memory_space=pltpu.SMEM)
    vmem = pl.BlockSpec(memory_space=pltpu.VMEM)

    def spec(value):
        return smem if len(value.shape) == 1 or value.dtype == jnp.int32 else vmem

    return pl.pallas_call(
        kernel,
        out_shape=outputs,
        in_specs=[spec(value) for value in inputs],
        out_specs=[spec(value) for value in outputs],
        scratch_shapes=scratch,
        input_output_aliases=aliases or {},
        compiler_params=pltpu.CompilerParams(vmem_limit_bytes=40 * 1024 * 1024),
        cost_estimate=pl.CostEstimate(flops=flops, bytes_accessed=0, transcendentals=0),
        name=name,
    )(*inputs)


def shards(positions, strengths, radius, block_count, pair_target, pair_slot, pair_count):
    blocks = block_count.shape[0]
    length = pair_target.shape[1]
    members = lax.axis_size("across")
    shard = lax.axis_index("blk")
    count = lax.axis_size("blk")

    def f32(*shape):
        return jax.ShapeDtypeStruct(shape, jnp.float32)

    def i32(*shape):
        return jax.ShapeDtypeStruct(shape, jnp.int32)

    (own,) = call(
        pack_kernel,
        "pack",
        (block_count, positions, strengths, radius.reshape(blocks, BLOCK)),
        [f32(SENT * blocks, BLOCK)],
        [],
    )
    paired = moved(own, "blk", to_paired_chip)
    others = [
        moved(own, "across", lambda source: (source - away) % members) for away in range(1, members)
    ]
    partner = moved(own, "blk", to_other_core)
    passed = moved(paired, "blk", along_chips(count))
    core = shard % 2
    chip = shard // 2 % 2
    crossed = moved(jnp.where(core == chip, paired, passed), "blk", to_other_core)

    state_shapes = [
        f32(members * blocks * ROWS, BLOCK),
        jax.ShapeDtypeStruct((members * blocks, BLOCK, FEATURES), jnp.bfloat16),
        f32(members * blocks * ROWS, BLOCK),
        f32(members * blocks * 2 * ROWS, BLOCK),
    ]
    window_shape = f32((2 * REACH + 1) * blocks * ROWS, BLOCK)
    list_shapes = [i32((CLASSES + 1) * length), i32((CLASSES + 1) * length), i32(CLASSES)]
    feature_rows = pltpu.VMEM((GROUP * FEATURES, BLOCK), jnp.float32)
    scratch = [
        pltpu.VMEM((GROUP * ROWS, BLOCK), jnp.float32),
        pltpu.VMEM((GROUP * 32, BLOCK), jnp.float32),
        pltpu.VMEM((GROUP * 2 * ROWS, BLOCK), jnp.float32),
    ]
    window_scratch = pltpu.VMEM(window_shape.shape, jnp.float32)

    def in_place(start, values=4):
        return {start + k: k for k in range(values)}

    results = call(
        home_kernel,
        "home_pairs",
        (pair_count, pair_target, pair_slot, own),
        list_shapes + state_shapes,
        [feature_rows] + scratch,
        flops=HOME_FLOPS,
    )
    lists, state = results[:3], results[3:]
    state = call(
        lambda *refs: near_kernel(*refs, members=members),
        "near_pairs",
        (*lists, own, partner, *others, *state),
        state_shapes,
        [window_scratch, feature_rows] + scratch,
        in_place(4 + members),
        flops=NEAR_FLOPS,
    )
    *state, window, away_sums = call(
        far_kernel,
        "far_pairs",
        (*lists, paired, passed, crossed, *state),
        state_shapes + [window_shape, f32(members - 1, 6 * blocks, BLOCK)],
        scratch,
        in_place(6),
        flops=FAR_FLOPS,
    )
    returned = [
        moved(away_sums[away - 1], "across", lambda source: (source + away) % members)
        for away in range(1, members)
    ]
    *state, sums = call(
        last_kernel,
        "last_pairs",
        (*lists, window, *state),
        state_shapes + [f32(1, 6 * blocks, BLOCK)],
        scratch,
        in_place(4),
        flops=FAR_FLOPS,
    )
    wide = f32(3, blocks * BLOCK)
    return tuple(
        call(section_kernel, "section", (own, sums[0], *returned), [wide] * 4, [])
    )


def solution(mesh):
    whole = P(None, ("blk", "across"))
    line = P(("blk", "across"))
    return jax.shard_map(
        shards,
        mesh=mesh,
        in_specs=(whole, whole, line, line, P(("blk", "across"), None), P(("blk", "across"), None), line),
        out_specs=(whole, whole, whole, whole),
        check_vma=False,
    )
```

time: 58.9 us -> 65.7 us (1.12)
  the two profiles are of different devices: /device:TPU:29 before, /device:TPU:5 now
where the time goes in v3:
time: 65.7 us; the launch traced here: 66.5 us
  Pallas kernels  40.4 us (61%)
  local copies, waits for them, and re-layouts  12.8 us (19%)
  starting transfers between devices  8.69 us (13%)
  waiting for transfers between devices  3.16 us (5%)
  between operations  1.39 us (2%)
    pallas_call x6, Pallas kernels, call(): pl.pallas_call(kernel, out_shape=outputs, in_specs=[spec(value) for value...  40.4 us
    unnamed x20, local copies, waits for them, and re-layouts  12.8 us
    ppermute x6, starting transfers between devices, moved(): return lax.ppermute(value, axis, pairs)  8.69 us
    ppermute x6, waiting for transfers between devices, moved(): return lax.ppermute(value, axis, pairs)  3.16 us
  transfers between devices with their start and end apart: 6, of which 1 were waited for; matrix products, arithmetic and copies ran while one was open for 0% of the time, Pallas kernels for 47%

profile of v3, /device:TPU:5, one launch (start us, length us, event | category | flops | bytes accessed | tf_op | source)
XLA Modules:
  0.0 66.5 jit_solution(15893710386190499783)
XLA Ops:
  0.6 0.0 copy-start
  0.6 0.9 %copy-done = f32[3,8192]{1,0:T(4,128)S(1)} copy-done((f32[3,8192]{1,0:T(4,128)S(1)}, f32[3,8192]{1,0:T(4,128)}, u32[]{:S(2)}) %copy-start) | copy-done | bytes 98328
  1.5 0.0 copy-start.1
  1.5 0.9 %copy-done.1 = f32[3,8192]{1,0:T(4,128)S(1)} copy-done((f32[3,8192]{1,0:T(4,128)S(1)}, f32[3,8192]{1,0:T(4,128)}, u32[]{:S(2)}) %copy-start.1) | copy-done | bytes 98328
  2.4 0.0 copy-start.2
  2.4 0.8 %copy-done.2 = f32[8192]{0:T(1024)S(1)} copy-done((f32[8192]{0:T(1024)S(1)}, f32[8192]{0:T(1024)}, u32[]{:S(2)}) %copy-start.2) | copy-done | bytes 32792
  3.2 0.0 copy-start.3
  3.2 0.7 copy-done.3
  3.9 0.7 %pack.1.own.refs_3_.sent = f32[448,128]{1,0:T(8,128)S(1)} custom-call(s32[64]{0:T(128)S(1)} %copy-done.3, f32[3,8192]{1,0:T(4,128)S(1)} %copy-done, f32[3,8192]{1,0:T(4,128)S(1)} %copy-done.1, f32[64,128]{1,0:T(8,128)S(1)} %bitcast.4), custom_call_target="tpu_custom_call" | custom-call | tf_op jit(solution)/shard_map/pack/pallas_call | solution.py:384
  4.5 0.1 collective-permute-start
  4.6 1.4 %collective-permute-start.4 = (f32[448,128]{1,0:T(8,128)S(1)}, f32[448,128]{1,0:T(8,128)S(1)}, u32[]{:S(2)}, u32[]{:S(2)}) collective-permute-start(f32[448,128]{1,0:T(8,128)S(1)} %pack.1.own.refs_3_.sent), channel_id=1, source_target_pairs={{0,1},{1,0},{2,3},{3,2},{4,5},{5,4},{6,7},{7,6},{8,9},{9,8},{10,11... | collective-permute-start | bytes 688136 | tf_op jit(solution)/shard_map/ppermute | solution.py:22
  6.0 1.2 %collective-permute-start.3 = (f32[448,128]{1,0:T(8,128)S(1)}, f32[448,128]{1,0:T(8,128)S(1)}, u32[]{:S(2)}, u32[]{:S(2)}) collective-permute-start(f32[448,128]{1,0:T(8,128)S(1)} %pack.1.own.refs_3_.sent), channel_id=1, source_target_pairs={{0,2},{2,0},{4,6},{6,4},{8,10},{10,8},{12,14},{14,12},{16,18},{18,... | collective-permute-start | bytes 688136 | tf_op jit(solution)/shard_map/ppermute | solution.py:22
  7.9 3.1 %collective-permute-done.paired = f32[448,128]{1,0:T(8,128)S(1)} collective-permute-done((f32[448,128]{1,0:T(8,128)S(1)}, f32[448,128]{1,0:T(8,128)S(1)}, u32[]{:S(2)}, u32[]{:S(2)}) %collective-permute-start) | collective-permute-done | bytes 229408 | tf_op jit(solution)/shard_map/ppermute | solution.py:22
  11.1 3.3 %collective-permute-start.1 = (f32[448,128]{1,0:T(8,128)S(1)}, f32[448,128]{1,0:T(8,128)S(1)}, u32[]{:S(2)}, u32[]{:S(2)}) collective-permute-start(f32[448,128]{1,0:T(8,128)S(1)} %collective-permute-done.paired), channel_id=1, source_target_pairs={{0,8},{2,10},{4,28},{6,30},{8,16},{10,18},{12,4},{14,6},{16,24},{1... | collective-permute-start | bytes 688136 | tf_op jit(solution)/shard_map/ppermute | solution.py:22
  14.4 0.0 copy-start.4
  14.4 0.7 %copy-done.4 = s32[1,256]{1,0:T(1,128)S(1)} copy-done((s32[1,256]{1,0:T(1,128)S(1)}, s32[1,256]{1,0:T(1,128)}, u32[]{:S(2)}) %copy-start.4) | copy-done | bytes 1048
  15.1 0.0 copy-start.5
  15.1 0.7 %copy-done.5 = s32[1,256]{1,0:T(1,128)S(1)} copy-done((s32[1,256]{1,0:T(1,128)S(1)}, s32[1,256]{1,0:T(1,128)}, u32[]{:S(2)}) %copy-start.5) | copy-done | bytes 1048
  15.8 11.6 %home_pairs.1 = (s32[1280]{0:T(1024)S(1)}, s32[1280]{0:T(1024)S(1)}, s32[4]{0:T(128)S(1)}, f32[1024,128]{1,0:T(8,128)S(1)}, bf16[128,128,64]{2,1,0:T(8,128)(2,1)...) custom-call(s32[1]{0:T(128)S(6)} %copy.35.number, s32[1,256]{1,0:T(1,128)S(1)} %copy-done.4, ...), custom_call_target="tpu_custom_call" | custom-call | flops 10000000000 | tf_op jit(solution)/shard_map/home_pairs/pallas_call | solution.py:384
  27.4 0.0 copy-start.6
  27.4 1.9 %copy-done.6 = bf16[128,128,64]{2,1,0:T(8,128)(2,1)} copy-done((bf16[128,128,64]{2,1,0:T(8,128)(2,1)}, bf16[128,128,64]{2,1,0:T(8,128)(2,1)S(1)}, u32[]{:S(2)}) %copy-start.6) | copy-done | bytes 2097176
  29.4 0.0 collective-permute-done.1.passed
  29.4 0.1 collective-permute-start.2
  29.5 0.0 collective-permute-done.4.refs_5_
  29.5 0.0 collective-permute-done.3.refs_4_
  29.5 0.0 copy-start.7
  29.5 2.2 %copy-done.7 = bf16[128,128,64]{2,1,0:T(8,128)(2,1)S(1)} copy-done((bf16[128,128,64]{2,1,0:T(8,128)(2,1)S(1)}, bf16[128,128,64]{2,1,0:T(8,128)(2,1)}, u32[]{:S(2)}) %copy-start.7) | copy-done | bytes 2097176
  31.7 11.1 %near_pairs.1 = (f32[1024,128]{1,0:T(8,128)S(1)}, bf16[128,128,64]{2,1,0:T(8,128)(2,1)S(1)}, f32[1024,128]{1,0:T(8,128)S(1)}, f32[2048,128]{1,0:T(8,128)S(1)}) custom-call(s32[1280]{0:T(1024)S(1)} %get-tuple-element.22.refs_0_.target_list, ...), custom_call_target="tpu_custom_call", output_to_operand_aliasing={{0}: (6, {}), {1}: (7, {}), {2}: (8, {}), {3}: (9, {})} | custom-call | flops 10000000000 | tf_op jit(solution)/shard_map/near_pairs/pallas_call | solution.py:384
  42.8 0.0 copy-start.8
  42.8 2.0 %copy-done.8 = bf16[128,128,64]{2,1,0:T(8,128)(2,1)} copy-done((bf16[128,128,64]{2,1,0:T(8,128)(2,1)}, bf16[128,128,64]{2,1,0:T(8,128)(2,1)S(1)}, u32[]{:S(2)}) %copy-start.8) | copy-done | bytes 2097176
  44.8 0.0 collective-permute-done.2.crossed
  44.8 0.0 copy-start.9
  44.8 2.2 %copy-done.9 = bf16[128,128,64]{2,1,0:T(8,128)(2,1)S(1)} copy-done((bf16[128,128,64]{2,1,0:T(8,128)(2,1)S(1)}, bf16[128,128,64]{2,1,0:T(8,128)(2,1)}, u32[]{:S(2)}) %copy-start.9) | copy-done | bytes 2097176
  47.0 7.0 %far_pairs.1 = (f32[1024,128]{1,0:T(8,128)S(1)}, bf16[128,128,64]{2,1,0:T(8,128)(2,1)S(1)}, f32[1024,128]{1,0:T(8,128)S(1)}, f32[2048,128]{1,0:T(8,128)S(1)}, f3...) custom-call(s32[1280]{0:T(1024)S(1)} %get-tuple-element.22.refs_0_.t, ...), custom_call_target="tpu_custom_call", output_to_operand_aliasing={{0}: (6, {}), {1}: (7, {}), {2}: (8, {}), {3}: (9, {})} | custom-call | flops 10000000000 | tf_op jit(solution)/shard_map/far_pairs/pallas_call | solution.py:384
  54.0 2.6 %collective-permute-start.5 = (f32[384,128]{1,0:T(8,128)S(1)}, f32[384,128]{1,0:T(8,128)S(1)}, u32[]{:S(2)}, u32[]{:S(2)}) collective-permute-start(f32[384,128]{1,0:T(8,128)S(1)} %bitcast.5), channel_id=1, source_target_pairs={{0,1},{1,0},{2,3},{3,2},{4,5},{5,4},{6,7},{7,6},{8,9},{9,8},{10,11... | collective-permute-start | bytes 589832 | tf_op jit(solution)/shard_map/ppermute | solution.py:22
  56.5 8.8 %last_pairs.1 = (f32[1024,128]{1,0:T(8,128)S(1)}, bf16[128,128,64]{2,1,0:T(8,128)(2,1)S(1)}, f32[1024,128]{1,0:T(8,128)S(1)}, f32[2048,128]{1,0:T(8,128)S(1)}, f32[1,384,128]{2,1,0:T(8,128)S(1)}) custom-call(s32[1280]{0:T(1024)S(1)} %get-tuple-element.22.refs_0_.target_list, ...), custom_call_target="tpu_custom_call", output_to_operand_aliasing={{0}: (4, {}), {1}: (5, {}), {2}: (6, {}), {3}: (7, {})} | custom-call | flops 10000000000 | tf_op jit(solution)/shard_map/last_pairs/pallas_call | solution.py:384
  65.3 0.0 collective-permute-done.5.refs_0_
  65.3 1.1 %section.1 = (f32[3,8192]{1,0:T(4,128)}, f32[3,8192]{1,0:T(4,128)}, f32[3,8192]{1,0:T(4,128)}, f32[3,8192]{1,0:T(4,128)}) custom-call(f32[448,128]{1,0:T(8,128)S(1)} %pack.1.own.refs_3_.sent, f32[384,128]{1,0:T(8,128)S(1)} %bitcast.3, f32[384,128]{1,0:T(8,128)S(1)} %collective-permute-done.5.refs_0_), custom_call_target="tpu_custom_call" | custom-call | tf_op jit(solution)/shard_map/section/pallas_call | solution.py:384
  (1 shorter events, 0.0 us)
Async XLA Ops:
  0.6 0.9 %copy-start = (f32[3,8192]{1,0:T(4,128)S(1)}, f32[3,8192]{1,0:T(4,128)}, u32[]{:S(2)}) copy-start(f32[3,8192]{1,0:T(4,128)} %positions.1) | copy-start | bytes 294916
  1.5 0.9 %copy-start.1 = (f32[3,8192]{1,0:T(4,128)S(1)}, f32[3,8192]{1,0:T(4,128)}, u32[]{:S(2)}) copy-start(f32[3,8192]{1,0:T(4,128)} %strengths.1) | copy-start | bytes 294916
  2.4 0.8 %copy-start.2 = (f32[8192]{0:T(1024)S(1)}, f32[8192]{0:T(1024)}, u32[]{:S(2)}) copy-start(f32[8192]{0:T(1024)} %param.9) | copy-start | bytes 98308
  3.2 0.7 copy-start.3
  4.5 6.5 %collective-permute-start = (f32[448,128]{1,0:T(8,128)S(1)}, f32[448,128]{1,0:T(8,128)S(1)}, u32[]{:S(2)}, u32[]{:S(2)}) collective-permute-start(f32[448,128]{1,0:T(8,128)S(1)} %pack.1.own.refs_3_.sent), channel_id=1, source_target_pairs={{0,4},{2,6},{4,0},{6,2},{8,12},{10,14},{12,8},{14,10},{16,20},{18,... | collective-permute-start | bytes 688136 | tf_op jit(solution)/shard_map/ppermute | solution.py:22
  4.6 24.8 %collective-permute-start.4 = (f32[448,128]{1,0:T(8,128)S(1)}, f32[448,128]{1,0:T(8,128)S(1)}, u32[]{:S(2)}, u32[]{:S(2)}) collective-permute-start(f32[448,128]{1,0:T(8,128)S(1)} %pack.1.own.refs_3_.sent), channel_id=1, source_target_pairs={{0,1},{1,0},{2,3},{3,2},{4,5},{5,4},{6,7},{7,6},{8,9},{9,8},{10,11... | collective-permute-start | bytes 688136 | tf_op jit(solution)/shard_map/ppermute | solution.py:22
  6.0 23.4 %collective-permute-start.3 = (f32[448,128]{1,0:T(8,128)S(1)}, f32[448,128]{1,0:T(8,128)S(1)}, u32[]{:S(2)}, u32[]{:S(2)}) collective-permute-start(f32[448,128]{1,0:T(8,128)S(1)} %pack.1.own.refs_3_.sent), channel_id=1, source_target_pairs={{0,2},{2,0},{4,6},{6,4},{8,10},{10,8},{12,14},{14,12},{16,18},{18,... | collective-permute-start | bytes 688136 | tf_op jit(solution)/shard_map/ppermute | solution.py:22
  11.1 18.3 %collective-permute-start.1 = (f32[448,128]{1,0:T(8,128)S(1)}, f32[448,128]{1,0:T(8,128)S(1)}, u32[]{:S(2)}, u32[]{:S(2)}) collective-permute-start(f32[448,128]{1,0:T(8,128)S(1)} %collective-permute-done.paired), channel_id=1, source_target_pairs={{0,8},{2,10},{4,28},{6,30},{8,16},{10,18},{12,4},{14,6},{16,24},{1... | collective-permute-start | bytes 688136 | tf_op jit(solution)/shard_map/ppermute | solution.py:22
  14.4 0.7 %copy-start.4 = (s32[1,256]{1,0:T(1,128)S(1)}, s32[1,256]{1,0:T(1,128)}, u32[]{:S(2)}) copy-start(s32[1,256]{1,0:T(1,128)} %pair_target.1) | copy-start | bytes 3076
  15.1 0.7 %copy-start.5 = (s32[1,256]{1,0:T(1,128)S(1)}, s32[1,256]{1,0:T(1,128)}, u32[]{:S(2)}) copy-start(s32[1,256]{1,0:T(1,128)} %pair_slot.1) | copy-start | bytes 3076
  27.4 2.0 %copy-start.6 = (bf16[128,128,64]{2,1,0:T(8,128)(2,1)}, bf16[128,128,64]{2,1,0:T(8,128)(2,1)S(1)}, u32[]{:S(2)}) copy-start(bf16[128,128,64]{2,1,0:T(8,128)(2,1)S(1)} %get-tuple-element.26.refs_7_) | copy-start | bytes 6291460
  29.4 15.4 %collective-permute-start.2 = (f32[448,128]{1,0:T(8,128)S(1)}, f32[448,128]{1,0:T(8,128)S(1)}, u32[]{:S(2)}, u32[]{:S(2)}) collective-permute-start(f32[448,128]{1,0:T(8,128)S(1)} %broadcast_select_fusion), channel_id=1, source_target_pairs={{0,2},{2,0},{4,6},{6,4},{8,10},{10,8},{12,14},{14,12},{16,18},{18,... | collective-permute-start | bytes 688136 | tf_op jit(solution)/shard_map/ppermute | solution.py:22
  29.5 2.2 %copy-start.7 = (bf16[128,128,64]{2,1,0:T(8,128)(2,1)S(1)}, bf16[128,128,64]{2,1,0:T(8,128)(2,1)}, u32[]{:S(2)}) copy-start(bf16[128,128,64]{2,1,0:T(8,128)(2,1)} %copy-done.6) | copy-start | bytes 6291460
  42.8 2.0 %copy-start.8 = (bf16[128,128,64]{2,1,0:T(8,128)(2,1)}, bf16[128,128,64]{2,1,0:T(8,128)(2,1)S(1)}, u32[]{:S(2)}) copy-start(bf16[128,128,64]{2,1,0:T(8,128)(2,1)S(1)} %get-tuple-element.30.refs_1_) | copy-start | bytes 6291460
  44.8 2.2 %copy-start.9 = (bf16[128,128,64]{2,1,0:T(8,128)(2,1)S(1)}, bf16[128,128,64]{2,1,0:T(8,128)(2,1)}, u32[]{:S(2)}) copy-start(bf16[128,128,64]{2,1,0:T(8,128)(2,1)} %copy-done.8) | copy-start | bytes 6291460
  54.0 11.4 %collective-permute-start.5 = (f32[384,128]{1,0:T(8,128)S(1)}, f32[384,128]{1,0:T(8,128)S(1)}, u32[]{:S(2)}, u32[]{:S(2)}) collective-permute-start(f32[384,128]{1,0:T(8,128)S(1)} %bitcast.5), channel_id=1, source_target_pairs={{0,1},{1,0},{2,3},{3,2},{4,5},{5,4},{6,7},{7,6},{8,9},{9,8},{10,11... | collective-permute-start | bytes 589832 | tf_op jit(solution)/shard_map/ppermute | solution.py:22

commit v4 on v3

v4 whole, which is shorter than its diff:
```python
import jax
import jax.numpy as jnp
from jax import lax
from jax.experimental import pallas as pl
from jax.experimental.pallas import tpu as pltpu
from jax.sharding import PartitionSpec as P

BLOCK = 128
ROWS = 8
REACH = 2
GROUP = 8
HALF = 4
FEATURES = 64
CLASSES = 8

biot_factor = 0.07957747154594767
section_step = 0.05


def moved(value, axis, target_of):
    pairs = [(source, target_of(source)) for source in range(lax.axis_size(axis))]
    return lax.ppermute(value, axis, pairs)


def to_other_core(source):
    return source ^ 1


def to_paired_chip(source):
    return source ^ 2


def along_chips(count):
    return lambda source: (source + (4 if source & 2 == 0 else -4)) % count


HOME_FLOPS = 10**10
NEAR_FLOPS = 10**10
FAR_FLOPS = 10**10


def rounded(value):
    return value.astype(jnp.bfloat16).astype(jnp.float32)


def split_three(value):
    first = rounded(value)
    rest = value - first
    second = rounded(rest)
    return first, second, rest - second


def cross(left, right):
    return [
        left[1] * right[2] - left[2] * right[1],
        left[2] * right[0] - left[0] * right[2],
        left[0] * right[1] - left[1] * right[0],
    ]


def tile_rows(index, rows):
    return pl.ds(pl.multiple_of(index * rows, rows), rows)


def component(ref, base, number, stride):
    return ref[pl.ds(base + number, GROUP, stride=stride), :]


def store_component(ref, base, number, stride, value):
    ref[pl.ds(base + number, GROUP, stride=stride), :] = value


def target_features(targets, step, centres, rows):
    base = pl.multiple_of(step * (GROUP * ROWS), GROUP * ROWS)
    pos = [component(targets, base, k, ROWS) for k in range(3)]
    strength = [component(targets, base, 3 + k, ROWS) for k in range(3)]
    for k in range(3):
        centre = jnp.broadcast_to(jnp.mean(pos[k], axis=1, keepdims=True), (GROUP, BLOCK))
        store_component(centres, base, k, ROWS, centre)
        pos[k] = pos[k] - centre
    for k in range(3, ROWS):
        store_component(centres, base, k, ROWS, jnp.zeros_like(pos[0]))
    norm = pos[0] * pos[0] + pos[1] * pos[1] + pos[2] * pos[2]
    own = pos[0] * strength[0] + pos[1] * strength[1] + pos[2] * strength[2]
    near = pos + [norm, jnp.ones_like(norm)]
    tilt = [0.5 * s for s in strength] + [own]
    for start, values in ((0, near), (32, tilt)):
        for k, value in enumerate(values):
            parts = split_three(value)
            for slot, part in enumerate((0, 1, 2, 0, 1, 0)):
                store_component(rows, 0, start + 5 * slot + k, BLOCK, parts[part])


def source_features(gathered, weight, left, charge):
    pos = [component(gathered, 0, k, ROWS) for k in range(3)]
    strength = [component(gathered, 0, 3 + k, ROWS) for k in range(3)]
    inv_core = 1.0 / component(gathered, 0, 6, ROWS)
    inv_square = inv_core * inv_core
    norm = pos[0] * pos[0] + pos[1] * pos[1] + pos[2] * pos[2]
    twice = -2.0 * inv_square
    shape = [p * twice for p in pos] + [inv_square, norm * inv_square + 1.0]
    for k, value in enumerate(shape):
        parts = split_three(value)
        for slot, part in enumerate((0, 0, 0, 1, 1, 2)):
            store_component(left, 0, 5 * slot + k, 32, parts[part])
    scale = inv_square * inv_core * weight
    for k, value in enumerate(strength + cross(pos, strength)):
        value = value * scale
        high = rounded(value)
        store_component(charge, 0, k, 2 * ROWS, high)
        store_component(charge, 0, ROWS + k, 2 * ROWS, value - high)


NT = (((1,), (1,)), ((), ()))


def put_tiles(window, first, tiles):
    window[pl.ds(pl.multiple_of(first * ROWS, ROWS), tiles.shape[0]), :] = tiles[...]


def prepare_targets(state, eye, feature_rows):
    targets, features, centres, total = state
    feature_rows[...] = jnp.zeros_like(feature_rows)

    def prepare(step, carry):
        target_features(targets, step, centres, feature_rows)
        for first in range(0, GROUP, 4):
            rows = feature_rows[first * BLOCK : (first + 4) * BLOCK, :].astype(jnp.bfloat16)
            turned = lax.dot_general(eye, rows, NT, preferred_element_type=jnp.float32)
            for u in range(4):
                part = turned[:, u * BLOCK : u * BLOCK + FEATURES]
                features[step * GROUP + first + u] = part.astype(jnp.bfloat16)
        wide = pl.ds(pl.multiple_of(step * GROUP * 2 * ROWS, GROUP * 2 * ROWS), GROUP * 2 * ROWS)
        total[wide, :] = jnp.zeros((GROUP * 2 * ROWS, BLOCK), jnp.float32)
        return carry

    lax.fori_loop(0, features.shape[0] // GROUP, prepare, 0)


def unit_matrix():
    row = lax.broadcasted_iota(jnp.int32, (BLOCK, BLOCK), 0)
    column = lax.broadcasted_iota(jnp.int32, (BLOCK, BLOCK), 1)
    return jnp.where(row == column, 1.0, 0.0).astype(jnp.bfloat16)


def run_class(kind, lists, window, state, scratch):
    _, features, centres, total = state
    gathered, left, charge_next, charge, first_half, second_half = scratch
    listed = lists[2 * ROWS + kind, 0]

    def entry_at(step, u):
        entry = jnp.minimum(step * GROUP + u, listed - 1)
        return entry // BLOCK * (3 * ROWS) + kind, lax.rem(entry, BLOCK)

    def target_of(step, u):
        row, column = entry_at(step, u)
        return lists[row, column]

    def prepare_sources(step):
        for u in range(GROUP):
            row, column = entry_at(step, u)
            gathered[u * ROWS : (u + 1) * ROWS, :] = (
                window[tile_rows(lists[row + ROWS, column], ROWS), :]
                - centres[tile_rows(lists[row, column], ROWS), :]
            )
        order = lax.broadcasted_iota(jnp.int32, (GROUP, BLOCK), 0) + step * GROUP
        weight = jnp.where(order < listed, 1.0, 0.0).astype(jnp.float32)
        source_features(gathered, weight, left, charge_next)

    def products(step, u, held):
        shape = left[u * 32 : (u + 1) * 32, :].astype(jnp.bfloat16)
        blank = jnp.zeros_like(shape)
        shape = jnp.concatenate(
            [jnp.concatenate([shape, blank], axis=1), jnp.concatenate([blank, shape], axis=1)],
            axis=0,
        )
        held[u % HALF] = jnp.dot(
            features[target_of(step, u)], shape, preferred_element_type=jnp.float32
        )

    def weights(u, held):
        near = held[u % HALF, :, :BLOCK]
        tilt = held[u % HALF, :, BLOCK:]
        q = lax.rsqrt(near)
        q2 = q * q
        q3 = q2 * q
        f = q3 * (q2 + (2.0 / 3.0))
        h = (q3 * q2) * (q2 + 0.4) * tilt
        fh = f.astype(jnp.bfloat16)
        fl = (f - fh.astype(jnp.float32)).astype(jnp.bfloat16)
        hh = h.astype(jnp.bfloat16)
        hl = (h - hh.astype(jnp.float32)).astype(jnp.bfloat16)
        return jnp.concatenate([fh, fl, hh, hl], axis=0)

    def add_up(step, u, stacked):
        pair = charge[u * 2 * ROWS : (u + 1) * 2 * ROWS, :]
        sums = lax.dot_general(pair, stacked, NT, preferred_element_type=jnp.float32)
        fsum = sums[0:8, 0:128] + sums[8:16, 0:128] + sums[0:8, 128:256]
        hsum = sums[0:8, 256:384] + sums[8:16, 256:384] + sums[0:8, 384:512]
        total[tile_rows(target_of(step, u), 2 * ROWS), :] += jnp.concatenate([fsum, hsum], axis=0)

    def turn(step, carry):
        stacked = {}
        for u in range(HALF):
            stacked[u] = weights(u, first_half)
            products(step, HALF + u, second_half)
            add_up(step, u, stacked[u])
        prepare_sources(step + 1)
        for u in range(HALF, GROUP):
            stacked[u] = weights(u, second_half)
            products(step + 1, u - HALF, first_half)
            add_up(step, u, stacked[u])
        charge[...] = charge_next[...].astype(jnp.bfloat16)
        return carry

    @pl.when(listed > 0)
    def _():
        left[...] = jnp.zeros_like(left)
        charge_next[...] = jnp.zeros_like(charge_next)
        prepare_sources(0)
        for u in range(HALF):
            products(0, u, first_half)
        charge[...] = charge_next[...].astype(jnp.bfloat16)
        lax.fori_loop(0, (listed + GROUP - 1) // GROUP, turn, 0)


def finish(state, out_ref):
    targets, _, centres, total = state
    blocks = out_ref.shape[1] // 6

    def one(step, carry):
        base = pl.multiple_of(step * GROUP * ROWS, GROUP * ROWS)
        wide = pl.multiple_of(step * GROUP * 2 * ROWS, GROUP * 2 * ROWS)
        pos = [
            component(targets, base, k, ROWS) - component(centres, base, k, ROWS) for k in range(3)
        ]
        strength = [component(targets, base, 3 + k, ROWS) for k in range(3)]
        fa, fb, ha, hb = [
            [component(total, wide, start + k, 2 * ROWS) for k in range(3)] for start in (0, 3, 8, 11)
        ]
        swirl = cross(pos, fa)
        lean = cross(strength, fa)
        bend = cross(pos, ha)
        member = step * GROUP // blocks
        inside = lax.rem(step * GROUP, blocks)
        for k in range(3):
            velocity = (-1.5 * biot_factor) * (swirl[k] - fb[k])
            stretch = (-1.5 * biot_factor) * lean[k] + (7.5 * biot_factor) * (bend[k] - hb[k])
            out_ref[member, pl.ds(pl.multiple_of(k * blocks + inside, GROUP), GROUP), :] = velocity
            out_ref[member, pl.ds(pl.multiple_of((3 + k) * blocks + inside, GROUP), GROUP), :] = stretch
        return carry

    lax.fori_loop(0, targets.shape[0] // ROWS // GROUP, one, 0)


def fetched(copies):
    for copy in copies:
        copy.start()
    for copy in copies:
        copy.wait()


def sort_list(listed, pair_target, pair_slot, sorted_list, blocks, members):
    length = pair_target.shape[1]
    t = pair_target[...]
    s = pair_slot[...]
    t = t - lax.axis_index("across") * blocks
    t = jnp.where(t < 0, t + members * blocks, t)
    partner = jnp.where(lax.axis_index("blk") % 2 == 0, REACH + 1, REACH - 1)
    run = s // blocks
    mine = t < blocks
    t = jnp.where(mine, t, t - blocks)
    home = run == REACH
    near = home | (run == partner)
    kind = jnp.where(
        near, jnp.where(mine, jnp.where(home, 0, 1), 2), jnp.where(mine, 4, 3)
    )
    entry = lax.broadcasted_iota(jnp.int32, (1, length), 1)
    kind = jnp.where(entry < listed, kind, CLASSES - 1)
    member = jnp.where(lax.broadcasted_iota(jnp.int32, (CLASSES, length), 0) == kind, 1.0, 0.0)
    row = lax.broadcasted_iota(jnp.int32, (length, length), 0)
    column = lax.broadcasted_iota(jnp.int32, (length, length), 1)
    before = jnp.where(row < column, 1.0, 0.0).astype(jnp.bfloat16)
    earlier = jnp.dot(member.astype(jnp.bfloat16), before, preferred_element_type=jnp.float32)
    rank = jnp.sum(member * earlier, axis=0, keepdims=True).astype(jnp.int32)
    place = jnp.where(row == rank, 1.0, 0.0).astype(jnp.bfloat16)
    values = [t // BLOCK, t % BLOCK, s // BLOCK, s % BLOCK]
    values = [member * value.astype(jnp.float32) for value in values]
    values = jnp.concatenate(values, axis=0).astype(jnp.bfloat16)
    found = lax.dot_general(values, place, NT, preferred_element_type=jnp.float32)
    number = jnp.broadcast_to(jnp.sum(member, axis=1, keepdims=True), (CLASSES, BLOCK))
    for j in range(length // BLOCK):
        part = found[:, j * BLOCK : (j + 1) * BLOCK]
        high, low = part[0:8], part[8:16]
        slot_high, slot_low = part[16:24], part[24:32]
        rows = [high * BLOCK + low, slot_high * BLOCK + slot_low, number]
        sorted_list[j * 24 : (j + 1) * 24, :] = jnp.concatenate(rows, axis=0).astype(jnp.int32)


class shifted_window:
    def __init__(self, ref, start):
        self.ref, self.start = ref, start * ROWS

    def __getitem__(self, index):
        rows, lanes = index
        return self.ref[pl.ds(pl.multiple_of(rows.start - self.start, ROWS), rows.size), lanes]


def home_kernel(number, pair_target, pair_slot, own, *refs, members):
    sorted_list, features, centres, total = refs[:4]
    feature_rows, list_in, slot_in, count_in, lists, sems = refs[4:10]
    scratch = refs[10:]
    state = (own, features, centres, total)
    blocks = own.shape[0] // ROWS
    pairs = ((number, count_in), (pair_target, list_in), (pair_slot, slot_in))
    fetched([pltpu.make_async_copy(a, b, sems.at[k]) for k, (a, b) in enumerate(pairs)])
    sort_list(count_in[0], list_in, slot_in, sorted_list, blocks, members)
    to_scalars = pltpu.make_async_copy(sorted_list, lists, sems.at[3])
    to_scalars.start()
    prepare_targets(state, unit_matrix(), feature_rows)
    to_scalars.wait()
    run_class(0, lists, shifted_window(own, REACH * blocks), state, scratch)


def side_of_partner():
    return jnp.where(lax.axis_index("blk") % 2 == 0, REACH + 1, REACH - 1)


def near_kernel(sorted_list, own, partner, *refs, members):
    others, refs = refs[: members - 1], refs[members - 1 :]
    targets, features, centres, total = state = refs[:4]
    window, feature_rows, lists, sems = refs[4:8]
    scratch = refs[8:]
    to_scalars = pltpu.make_async_copy(sorted_list, lists, sems.at[0])
    to_scalars.start()
    blocks = own.shape[0] // ROWS
    put_tiles(window, REACH * blocks, own)
    put_tiles(window, side_of_partner() * blocks, partner)
    for r, other in enumerate(others):
        put_tiles(targets, r * blocks, other)
    prepare_targets(state, unit_matrix(), feature_rows)
    to_scalars.wait()
    run_class(2, lists, window, state, scratch)


def partner_kernel(sorted_list, partner, own, features, centres, _, total, lists, sems, *scratch):
    fetched([pltpu.make_async_copy(sorted_list, lists, sems.at[0])])
    window = shifted_window(partner, side_of_partner() * (partner.shape[0] // ROWS))
    run_class(1, lists, window, (own, features, centres, total), scratch)


def far_kernel(sorted_list, paired, passed, crossed, *refs):
    targets, features, centres, _ = refs[:4]
    total, window, out_ref = refs[4:7]
    lists, sems = refs[7:9]
    scratch = refs[9:]
    state = (targets, features, centres, total)
    to_scalars = pltpu.make_async_copy(sorted_list, lists, sems.at[0])
    to_scalars.start()
    blocks = paired.shape[0] // ROWS
    shard = lax.axis_index("blk")
    even = shard // 2 % 2 == 0
    put_tiles(window, jnp.where(even, 2 * REACH, 0) * blocks, paired)
    put_tiles(window, jnp.where(even, 0, 2 * REACH) * blocks, passed)
    put_tiles(window, jnp.where(shard % 2 == 0, REACH - 1, REACH + 1) * blocks, crossed)
    to_scalars.wait()
    run_class(3, lists, window, state, scratch)
    finish(state, out_ref)


def last_kernel(sorted_list, window, own, features, centres, _, total, out_ref, lists, sems, *scratch):
    state = (own, features, centres, total)
    fetched([pltpu.make_async_copy(sorted_list, lists, sems.at[0])])
    run_class(4, lists, window, state, scratch)
    finish(state, out_ref)


def section_kernel(own, sums, *refs):
    returned, (velocity, stretching, section_positions, section_strengths) = refs[:-4], refs[-4:]
    blocks = own.shape[0] // ROWS
    for b in range(blocks):
        lanes = slice(b * BLOCK, (b + 1) * BLOCK)
        for start, result, stepped in ((0, velocity, section_positions), (3, stretching, section_strengths)):
            chosen = pl.ds(start * blocks + b, 3, stride=blocks)
            value = sums[chosen, :]
            for other in returned:
                value = value + other[chosen, :]
            result[:, lanes] = value
            first = b * ROWS + start
            stepped[:, lanes] = own[first : first + 3, :] + section_step * value


def call(kernel, name, inputs, outputs, scratch, aliases=None, far=0, flops=0):
    vmem = pl.BlockSpec(memory_space=pltpu.VMEM)
    hbm = pl.BlockSpec(memory_space=pltpu.HBM)
    held = sum(value.size * value.dtype.itemsize for value in (*inputs, *outputs))
    return pl.pallas_call(
        kernel,
        out_shape=outputs,
        in_specs=[hbm if k < far else vmem for k in range(len(inputs))],
        out_specs=[vmem for value in outputs],
        scratch_shapes=scratch,
        input_output_aliases=aliases or {},
        compiler_params=pltpu.CompilerParams(vmem_limit_bytes=10 * 1024 * 1024 + 2 * held),
        cost_estimate=pl.CostEstimate(flops=flops, bytes_accessed=0, transcendentals=0),
        name=name,
    )(*inputs)


def shards(positions, strengths, radius, block_count, pair_target, pair_slot, pair_count):
    blocks = block_count.shape[0]
    lanes = blocks * BLOCK
    length = pair_target.shape[1]
    members = lax.axis_size("across")
    shard = lax.axis_index("blk")
    count = lax.axis_size("blk")

    def f32(*shape):
        return jax.ShapeDtypeStruct(shape, jnp.float32)

    slot_index = lax.broadcasted_iota(jnp.int32, (blocks, 3, BLOCK), 2)
    live = jnp.where(
        slot_index < block_count[:, None, None],
        strengths.reshape(3, blocks, BLOCK).transpose(1, 0, 2),
        0.0,
    )
    cores = radius.reshape(blocks, 1, BLOCK)
    own = jnp.concatenate(
        [positions.reshape(3, blocks, BLOCK).transpose(1, 0, 2), live, cores, cores], axis=1
    ).reshape(blocks * ROWS, BLOCK)
    paired = moved(own, "blk", to_paired_chip)
    others = [
        moved(own, "across", lambda source: (source - away) % members) for away in range(1, members)
    ]
    partner = moved(own, "blk", to_other_core)

    def state_shapes(number):
        return [
            f32(number * blocks * ROWS, BLOCK),
            jax.ShapeDtypeStruct((number * blocks, BLOCK, FEATURES), jnp.bfloat16),
            f32(number * blocks * ROWS, BLOCK),
            f32(number * blocks * 2 * ROWS, BLOCK),
        ]

    own_shapes, other_shapes = state_shapes(1), state_shapes(members - 1)
    window_shape = f32((2 * REACH + 1) * blocks * ROWS, BLOCK)
    list_shape = jax.ShapeDtypeStruct((3 * ROWS * length // BLOCK, BLOCK), jnp.int32)
    feature_rows = pltpu.VMEM((GROUP * BLOCK, BLOCK), jnp.float32)
    list_scratch = [pltpu.SMEM(list_shape.shape, jnp.int32), pltpu.SemaphoreType.DMA((4,))]
    scratch = [
        pltpu.VMEM((GROUP * ROWS, BLOCK), jnp.float32),
        pltpu.VMEM((GROUP * 32, BLOCK), jnp.float32),
        pltpu.VMEM((GROUP * 2 * ROWS, BLOCK), jnp.float32),
        pltpu.VMEM((GROUP * 2 * ROWS, BLOCK), jnp.bfloat16),
        pltpu.VMEM((HALF, BLOCK, 2 * BLOCK), jnp.float32),
        pltpu.VMEM((HALF, BLOCK, 2 * BLOCK), jnp.float32),
    ]
    window_scratch = pltpu.VMEM(window_shape.shape, jnp.float32)

    lists, *own_state = call(
        lambda *refs: home_kernel(*refs, members=members),
        "home_pairs",
        (pair_count, pair_target, pair_slot, own),
        [list_shape] + own_shapes[1:],
        [
            feature_rows,
            pltpu.VMEM((1, length), jnp.int32),
            pltpu.VMEM((1, length), jnp.int32),
            pltpu.SMEM((1,), jnp.int32),
        ]
        + list_scratch
        + scratch,
        far=3,
        flops=HOME_FLOPS,
    )
    paired, lists = lax.optimization_barrier((paired, lists))
    passed = moved(paired, "blk", along_chips(count))
    other_state = list(call(
        lambda *refs: near_kernel(*refs, members=members),
        "near_pairs",
        (lists, own, partner, *others),
        other_shapes,
        [window_scratch, feature_rows] + list_scratch + scratch,
        flops=NEAR_FLOPS,
    ))
    passed, other_state[3] = lax.optimization_barrier((passed, other_state[3]))
    core = shard % 2
    chip = shard // 2 % 2
    crossed = moved(jnp.where(core == chip, paired, passed), "blk", to_other_core)
    (own_state[2],) = call(
        partner_kernel,
        "partner_pairs",
        (lists, partner, own, *own_state),
        [own_shapes[3]],
        list_scratch + scratch,
        {5: 0},
        flops=HOME_FLOPS,
    )
    crossed, own_state[2] = lax.optimization_barrier((crossed, own_state[2]))
    _, window, away_sums = call(
        far_kernel,
        "far_pairs",
        (lists, paired, passed, crossed, *other_state),
        [other_shapes[3], window_shape, f32(members - 1, 6 * blocks, BLOCK)],
        list_scratch + scratch,
        {7: 0},
        flops=FAR_FLOPS,
    )
    returned = [
        moved(away_sums[away - 1], "across", lambda source: (source + away) % members)
        for away in range(1, members)
    ]
    _, sums = call(
        last_kernel,
        "last_pairs",
        (lists, window, own, *own_state),
        [own_shapes[3], f32(1, 6 * blocks, BLOCK)],
        list_scratch + scratch,
        {5: 0},
        flops=FAR_FLOPS,
    )
    wide = f32(3, lanes)
    return tuple(
        call(section_kernel, "section", (own, sums[0], *returned), [wide] * 4, [])
    )


def solution(mesh):
    whole = P(None, ("blk", "across"))
    line = P(("blk", "across"))
    return jax.shard_map(
        shards,
        mesh=mesh,
        in_specs=(whole, whole, line, line, P(("blk", "across"), None), P(("blk", "across"), None), line),
        out_specs=(whole, whole, whole, whole),
        check_vma=False,
    )
```

time: 65.7 us -> 47.9 us (0.73)
  the two profiles are of different devices: /device:TPU:5 before, /device:TPU:0 now
where the time goes in v4:
time: 47.9 us; the launch traced here: 47.3 us
  Pallas kernels  34.9 us (73%)
  starting transfers between devices  6.72 us (14%)
  local copies, waits for them, and re-layouts  2.15 us (4%)
  other arithmetic  2.14 us (4%)
  between operations  1.39 us (3%)
    pallas_call x6, Pallas kernels, call(): pl.pallas_call(kernel, out_shape=outputs, in_specs=[hbm if k < far else v...  34.9 us
    ppermute x6, starting transfers between devices, moved(): return lax.ppermute(value, axis, pairs)  6.72 us
    unnamed x8, local copies, waits for them, and re-layouts  2.15 us
    reshape x1, other arithmetic, shards(): own = jnp.concatenate([positions.reshape(3, blocks, BLOCK).transpose(1, 0...  1.07 us
    select_n x1, other arithmetic, shards(): jnp.where(slot_index < block_count[:, None, None], strengths.reshape(3, b...  1.04 us
  transfers between devices with their start and end apart: 6, of which 1 were waited for; matrix products, arithmetic and copies ran while one was open for 0% of the time, Pallas kernels for 54%

profile of v4, /device:TPU:0, one launch (start us, length us, event | category | flops | bytes accessed | tf_op | source)
XLA Modules:
  0.0 47.3 jit_solution(4067022485249180925)
XLA Ops:
  0.6 1.0 %bitcast_select_fusion = f32[64,3,128]{2,1,0:T(4,128)S(1)} fusion(f32[3,8192]{1,0:T(4,128)} %param.8, s32[64]{0:T(128)} %param.10), kind=kLoop, calls=%fused_computation.1 | loop fusion | flops 49152 | bytes 196864 | tf_op jit(solution)/shard_map/jit(_where)/select_n | solution.py:422
  1.7 1.1 %maximum_bitcast_fusion.refs_3_.refs_1_.own = f32[512,128]{1,0:T(8,128)S(1)} fusion(f32[64,1,128]{2,1,0:T(1,128)} %bitcast.15, f32[64,3,128]{2,1,0:T(4,128)S(1)} %bitcast_select_fusion, f32[64,3,128]{2,1,0:T(4,128)} %bitcast.14), kind=kLoop, calls=%fused_computation | loop fusion | flops 196608 | bytes 491520 | tf_op jit(solution)/shard_map/reshape | solution.py:430
  2.7 3.0 %collective-permute-start.3 = (f32[512,128]{1,0:T(8,128)S(1)}, f32[512,128]{1,0:T(8,128)S(1)}, u32[]{:S(2)}, u32[]{:S(2)}) collective-permute-start(f32[512,128]{1,0:T(8,128)S(1)} %maximum_bitcast_fusion.refs_3_.refs_1_.own), channel_id=1, source_target_pairs={{0,1},{1,0},{2,3},{3,2},{4,5},{5,4},{6,7},{7,6},{8,9},{9,8},{10,11... | collective-permute-start | bytes 786440 | tf_op jit(solution)/shard_map/ppermute | solution.py:22
  5.8 0.0 collective-permute-start.2
  5.8 1.5 %collective-permute-start = (f32[512,128]{1,0:T(8,128)S(1)}, f32[512,128]{1,0:T(8,128)S(1)}, u32[]{:S(2)}, u32[]{:S(2)}) collective-permute-start(f32[512,128]{1,0:T(8,128)S(1)} %maximum_bitcast_fusion.refs_3_.refs_1_.own), channel_id=1, source_target_pairs={{0,4},{2,6},{4,0},{6,2},{8,12},{10,14},{12,8},{14,10},{16,20},{18,... | collective-permute-start | bytes 786440 | tf_op jit(solution)/shard_map/ppermute | solution.py:22
  7.9 0.0 copy-start
  7.9 0.7 %copy-done = s32[1,256]{1,0:T(1,128)S(1)} copy-done((s32[1,256]{1,0:T(1,128)S(1)}, s32[1,256]{1,0:T(1,128)}, u32[]{:S(2)}) %copy-start) | copy-done | bytes 1048
  8.6 0.0 copy-start.1
  8.6 0.7 %copy-done.1 = s32[1,256]{1,0:T(1,128)S(1)} copy-done((s32[1,256]{1,0:T(1,128)S(1)}, s32[1,256]{1,0:T(1,128)}, u32[]{:S(2)}) %copy-start.1) | copy-done | bytes 1048
  9.3 6.4 %home_pairs.1 = (s32[48,128]{1,0:T(8,128)S(1)}, bf16[64,128,64]{2,1,0:T(8,128)(2,1)S(1)}, f32[512,128]{1,0:T(8,128)S(1)}, f32[1024,128]{1,0:T(8,128)S(1)}) custom-call(s32[1]{0:T(128)S(6)} %copy.19.refs_0_, s32[1,256]{1,0:T(1,128)S(1)} %copy-done, s32[1,256]{1,0:T(1,128)S(1)} %copy-done.1, f32[512,128]{1,0:T(8,128)S(1)} %maximum_bitcast_fusion.refs_3_.refs_1_.own), custom_call_target="tpu_custom_call" | custom-call | flops 10000000000 | tf_op jit(solution)/shard_map/home_pairs/pallas_call | solution.py:397
  15.7 0.0 copy-start.2
  15.7 0.8 %copy-done.2 = f32[1024,128]{1,0:T(8,128)} copy-done((f32[1024,128]{1,0:T(8,128)}, f32[1024,128]{1,0:T(8,128)S(1)}, u32[]{:S(2)}) %copy-start.2) | copy-done | bytes 524312
  16.5 0.0 collective-permute-done.paired
  16.5 0.0 copy-start.3
  16.5 1.6 %collective-permute-start.1 = (f32[512,128]{1,0:T(8,128)S(1)}, f32[512,128]{1,0:T(8,128)S(1)}, u32[]{:S(2)}, u32[]{:S(2)}) collective-permute-start(f32[512,128]{1,0:T(8,128)S(1)} %collective-permute-done.paired), channel_id=1, source_target_pairs={{0,8},{2,10},{4,28},{6,30},{8,16},{10,18},{12,4},{14,6},{16,24},{1... | collective-permute-start | bytes 786440 | tf_op jit(solution)/shard_map/ppermute | solution.py:22
  18.1 0.0 collective-permute-done.3.refs_3_
  18.1 0.0 collective-permute-done.2.refs_2_.partner
  18.1 7.4 %near_pairs.1 = (f32[512,128]{1,0:T(8,128)S(1)}, bf16[64,128,64]{2,1,0:T(8,128)(2,1)S(1)}, f32[512,128]{1,0:T(8,128)S(1)}, f32[1024,128]{1,0:T(8,128)S(1)}) custom-call(s32[48,128]{1,0:T(8,128)S(1)} %get-tuple-element.22.refs_0_.sorted_list, f32[512,128]{1,0:T(8,128)S(1)} %maximum_bitcast_fusion.refs_3_.refs_1_.own, ...), custom_call_target="tpu_custom_call" | custom-call | flops 10000000000 | tf_op jit(solution)/shard_map/near_pairs/pallas_call | solution.py:397
  25.5 0.1 collective-permute-done.1.passed
  25.6 0.1 collective-permute-start.4
  25.7 0.0 copy-done.3
  25.7 3.8 %partner_pairs.1._ = f32[1024,128]{1,0:T(8,128)S(1)} custom-call(s32[48,128]{1,0:T(8,128)S(1)} %get-tuple-element.22.refs_0_.sorted_list, f32[512,128]{1,0:T(8,128)S(1)} %collective-permute-done.2.refs_2_.partner, f32[512,128]{1,0:T(8,128)S(1)} %maximum_bitcast_fusion.refs_3_.refs_1_.own, ...), custom_call_target="tpu_custom_call", output_to_operand_aliasing={{}: (5, {})} | custom-call | flops 10000000000 | tf_op jit(solution)/shard_map/partner_pairs/pallas_call | solution.py:397
  29.6 0.0 collective-permute-done.4.crossed
  29.6 8.3 %far_pairs.1 = (f32[1024,128]{1,0:T(8,128)S(1)}, f32[2560,128]{1,0:T(8,128)S(1)}, f32[1,384,128]{2,1,0:T(8,128)S(1)}) custom-call(s32[48,128]{1,0:T(8,128)S(1)} %get-tuple-element.22.refs_0_.sorted_list, f32[512,128]{1,0:T(8,128)S(1)} %collective-permute-done.paired, f32[512,128]{1,0:T(8,128)S(1)} %collective-permute-done.1.passed, ...), custom_call_target="tpu_custom_call", output_to_operand_aliasing={{0}: (7, {})} | custom-call | flops 10000000000 | tf_op jit(solution)/shard_map/far_pairs/pallas_call | solution.py:397
  37.9 0.6 %collective-permute-start.5 = (f32[384,128]{1,0:T(8,128)S(1)}, f32[384,128]{1,0:T(8,128)S(1)}, u32[]{:S(2)}, u32[]{:S(2)}) collective-permute-start(f32[384,128]{1,0:T(8,128)S(1)} %bitcast.13), channel_id=1, source_target_pairs={{0,1},{1,0},{2,3},{3,2},{4,5},{5,4},{6,7},{7,6},{8,9},{9,8},{10,11... | collective-permute-start | bytes 589832 | tf_op jit(solution)/shard_map/ppermute | solution.py:22
  38.5 7.7 %last_pairs.1 = (f32[1024,128]{1,0:T(8,128)S(1)}, f32[1,384,128]{2,1,0:T(8,128)S(1)}) custom-call(s32[48,128]{1,0:T(8,128)S(1)} %get-tuple-element.22.refs_0_.sorted_list, f32[2560,128]{1,0:T(8,128)S(1)} %get-tuple-element.34.window, f32[512,128]{1,0:T(8,128)S(1)} %maximum_bitcast_fusion.refs_3_.refs_1_.own, ...), custom_call_target="tpu_custom_call", output_to_operand_aliasing={{0}: (5, {})} | custom-call | flops 10000000000 | tf_op jit(solution)/shard_map/last_pairs/pallas_call | solution.py:397
  46.2 0.0 collective-permute-done.5.refs_0_
  46.2 1.1 %section.1 = (f32[3,8192]{1,0:T(4,128)}, f32[3,8192]{1,0:T(4,128)}, f32[3,8192]{1,0:T(4,128)}, f32[3,8192]{1,0:T(4,128)}) custom-call(f32[512,128]{1,0:T(8,128)S(1)} %maximum_bitcast_fusion.refs_3_.refs_1_.own, f32[384,128]{1,0:T(8,128)S(1)} %bitcast.12, f32[384,128]{1,0:T(8,128)S(1)} %collective-permute-done.5.refs_0_), custom_call_target="tpu_custom_call" | custom-call | tf_op jit(solution)/shard_map/section/pallas_call | solution.py:397
  (1 shorter events, 0.0 us)
Async XLA Ops:
  2.7 15.3 %collective-permute-start.3 = (f32[512,128]{1,0:T(8,128)S(1)}, f32[512,128]{1,0:T(8,128)S(1)}, u32[]{:S(2)}, u32[]{:S(2)}) collective-permute-start(f32[512,128]{1,0:T(8,128)S(1)} %maximum_bitcast_fusion.refs_3_.refs_1_.own), channel_id=1, source_target_pairs={{0,1},{1,0},{2,3},{3,2},{4,5},{5,4},{6,7},{7,6},{8,9},{9,8},{10,11... | collective-permute-start | bytes 786440 | tf_op jit(solution)/shard_map/ppermute | solution.py:22
  5.8 12.3 %collective-permute-start.2 = (f32[512,128]{1,0:T(8,128)S(1)}, f32[512,128]{1,0:T(8,128)S(1)}, u32[]{:S(2)}, u32[]{:S(2)}) collective-permute-start(f32[512,128]{1,0:T(8,128)S(1)} %maximum_bitcast_fusion.refs_3_.refs_1_.own), channel_id=1, source_target_pairs={{0,2},{2,0},{4,6},{6,4},{8,10},{10,8},{12,14},{14,12},{16,18},{18,... | collective-permute-start | bytes 786440 | tf_op jit(solution)/shard_map/ppermute | solution.py:22
  5.8 10.8 %collective-permute-start = (f32[512,128]{1,0:T(8,128)S(1)}, f32[512,128]{1,0:T(8,128)S(1)}, u32[]{:S(2)}, u32[]{:S(2)}) collective-permute-start(f32[512,128]{1,0:T(8,128)S(1)} %maximum_bitcast_fusion.refs_3_.refs_1_.own), channel_id=1, source_target_pairs={{0,4},{2,6},{4,0},{6,2},{8,12},{10,14},{12,8},{14,10},{16,20},{18,... | collective-permute-start | bytes 786440 | tf_op jit(solution)/shard_map/ppermute | solution.py:22
  7.9 0.7 %copy-start = (s32[1,256]{1,0:T(1,128)S(1)}, s32[1,256]{1,0:T(1,128)}, u32[]{:S(2)}) copy-start(s32[1,256]{1,0:T(1,128)} %refs_1_.1) | copy-start | bytes 3076
  8.6 0.7 %copy-start.1 = (s32[1,256]{1,0:T(1,128)S(1)}, s32[1,256]{1,0:T(1,128)}, u32[]{:S(2)}) copy-start(s32[1,256]{1,0:T(1,128)} %refs_2_.1) | copy-start | bytes 3076
  15.7 0.8 %copy-start.2 = (f32[1024,128]{1,0:T(8,128)}, f32[1024,128]{1,0:T(8,128)S(1)}, u32[]{:S(2)}) copy-start(f32[1024,128]{1,0:T(8,128)S(1)} %get-tuple-element.28._) | copy-start | bytes 1572868
  16.5 9.2 %copy-start.3 = (f32[1024,128]{1,0:T(8,128)S(1)}, f32[1024,128]{1,0:T(8,128)}, u32[]{:S(2)}) copy-start(f32[1024,128]{1,0:T(8,128)} %copy-done.2) | copy-start | bytes 1572868
  16.5 9.1 %collective-permute-start.1 = (f32[512,128]{1,0:T(8,128)S(1)}, f32[512,128]{1,0:T(8,128)S(1)}, u32[]{:S(2)}, u32[]{:S(2)}) collective-permute-start(f32[512,128]{1,0:T(8,128)S(1)} %collective-permute-done.paired), channel_id=1, source_target_pairs={{0,8},{2,10},{4,28},{6,30},{8,16},{10,18},{12,4},{14,6},{16,24},{1... | collective-permute-start | bytes 786440 | tf_op jit(solution)/shard_map/ppermute | solution.py:22
  25.6 3.9 %collective-permute-start.4 = (f32[512,128]{1,0:T(8,128)S(1)}, f32[512,128]{1,0:T(8,128)S(1)}, u32[]{:S(2)}, u32[]{:S(2)}) collective-permute-start(f32[512,128]{1,0:T(8,128)S(1)} %broadcast_select_fusion), channel_id=1, source_target_pairs={{0,2},{2,0},{4,6},{6,4},{8,10},{10,8},{12,14},{14,12},{16,18},{18,... | collective-permute-start | bytes 786440 | tf_op jit(solution)/shard_map/ppermute | solution.py:22
  37.9 8.3 %collective-permute-start.5 = (f32[384,128]{1,0:T(8,128)S(1)}, f32[384,128]{1,0:T(8,128)S(1)}, u32[]{:S(2)}, u32[]{:S(2)}) collective-permute-start(f32[384,128]{1,0:T(8,128)S(1)} %bitcast.13), channel_id=1, source_target_pairs={{0,1},{1,0},{2,3},{3,2},{4,5},{5,4},{6,7},{7,6},{8,9},{9,8},{10,11... | collective-permute-start | bytes 589832 | tf_op jit(solution)/shard_map/ppermute | solution.py:22

commit v5 on v4

--- a/solution.py
+++ b/solution.py
@@ -10,7 +10,8 @@
 REACH = 2
 GROUP = 8
 HALF = 4
-FEATURES = 64
+SLOTS = 1024
+FEATURES = 32
 CLASSES = 8
 
 biot_factor = 0.07957747154594767
@@ -70,7 +71,7 @@
     ref[pl.ds(base + number, GROUP, stride=stride), :] = value
 
 
-def target_features(targets, step, centres, rows):
+def target_features(targets, step, centres, near_rows, tilt_rows):
     base = pl.multiple_of(step * (GROUP * ROWS), GROUP * ROWS)
     pos = [component(targets, base, k, ROWS) for k in range(3)]
     strength = [component(targets, base, 3 + k, ROWS) for k in range(3)]
@@ -84,11 +85,11 @@
     own = pos[0] * strength[0] + pos[1] * strength[1] + pos[2] * strength[2]
     near = pos + [norm, jnp.ones_like(norm)]
     tilt = [0.5 * s for s in strength] + [own]
-    for start, values in ((0, near), (32, tilt)):
+    for rows, values in ((near_rows, near), (tilt_rows, tilt)):
         for k, value in enumerate(values):
             parts = split_three(value)
             for slot, part in enumerate((0, 1, 2, 0, 1, 0)):
-                store_component(rows, 0, start + 5 * slot + k, BLOCK, parts[part])
+                store_component(rows, 0, 5 * slot + k, FEATURES, parts[part])
 
 
 def source_features(gathered, weight, left, charge):
@@ -102,7 +103,7 @@
     for k, value in enumerate(shape):
         parts = split_three(value)
         for slot, part in enumerate((0, 0, 0, 1, 1, 2)):
-            store_component(left, 0, 5 * slot + k, 32, parts[part])
+            store_component(left, 0, 5 * slot + k, FEATURES, parts[part])
     scale = inv_square * inv_core * weight
     for k, value in enumerate(strength + cross(pos, strength)):
         value = value * scale
@@ -112,35 +113,28 @@
 
 
 NT = (((1,), (1,)), ((), ()))
+TN = (((0,), (0,)), ((), ()))
 
 
 def put_tiles(window, first, tiles):
     window[pl.ds(pl.multiple_of(first * ROWS, ROWS), tiles.shape[0]), :] = tiles[...]
 
 
-def prepare_targets(state, eye, feature_rows):
+def prepare_targets(state, near_rows, tilt_rows):
     targets, features, centres, total = state
-    feature_rows[...] = jnp.zeros_like(feature_rows)
+    near_rows[...] = jnp.zeros_like(near_rows)
+    tilt_rows[...] = jnp.zeros_like(tilt_rows)
+    total[...] = jnp.zeros_like(total)
 
     def prepare(step, carry):
-        target_features(targets, step, centres, feature_rows)
-        for first in range(0, GROUP, 4):
-            rows = feature_rows[first * BLOCK : (first + 4) * BLOCK, :].astype(jnp.bfloat16)
-            turned = lax.dot_general(eye, rows, NT, preferred_element_type=jnp.float32)
-            for u in range(4):
-                part = turned[:, u * BLOCK : u * BLOCK + FEATURES]
-                features[step * GROUP + first + u] = part.astype(jnp.bfloat16)
-        wide = pl.ds(pl.multiple_of(step * GROUP * 2 * ROWS, GROUP * 2 * ROWS), GROUP * 2 * ROWS)
-        total[wide, :] = jnp.zeros((GROUP * 2 * ROWS, BLOCK), jnp.float32)
+        target_features(targets, step, centres, near_rows, tilt_rows)
+        for u in range(GROUP):
+            rows = slice(u * FEATURES, (u + 1) * FEATURES)
+            features[step * GROUP + u, :, :BLOCK] = near_rows[rows, :].astype(jnp.bfloat16)
+            features[step * GROUP + u, :, BLOCK:] = tilt_rows[rows, :].astype(jnp.bfloat16)
         return carry
 
     lax.fori_loop(0, features.shape[0] // GROUP, prepare, 0)
-
-
-def unit_matrix():
-    row = lax.broadcasted_iota(jnp.int32, (BLOCK, BLOCK), 0)
-    column = lax.broadcasted_iota(jnp.int32, (BLOCK, BLOCK), 1)
-    return jnp.where(row == column, 1.0, 0.0).astype(jnp.bfloat16)
 
 
 def run_class(kind, lists, window, state, scratch):
@@ -168,14 +162,9 @@
         source_features(gathered, weight, left, charge_next)
 
     def products(step, u, held):
-        shape = left[u * 32 : (u + 1) * 32, :].astype(jnp.bfloat16)
-        blank = jnp.zeros_like(shape)
-        shape = jnp.concatenate(
-            [jnp.concatenate([shape, blank], axis=1), jnp.concatenate([blank, shape], axis=1)],
-            axis=0,
-        )
-        held[u % HALF] = jnp.dot(
-            features[target_of(step, u)], shape, preferred_element_type=jnp.float32
+        shape = left[u * FEATURES : (u + 1) * FEATURES, :].astype(jnp.bfloat16)
+        held[u % HALF] = lax.dot_general(
+            shape, features[target_of(step, u)], TN, preferred_element_type=jnp.float32
         )
 
     def weights(u, held):
@@ -190,11 +179,11 @@
         fl = (f - fh.astype(jnp.float32)).astype(jnp.bfloat16)
         hh = h.astype(jnp.bfloat16)
         hl = (h - hh.astype(jnp.float32)).astype(jnp.bfloat16)
-        return jnp.concatenate([fh, fl, hh, hl], axis=0)
+        return jnp.concatenate([fh, fl, hh, hl], axis=1)
 
     def add_up(step, u, stacked):
         pair = charge[u * 2 * ROWS : (u + 1) * 2 * ROWS, :]
-        sums = lax.dot_general(pair, stacked, NT, preferred_element_type=jnp.float32)
+        sums = jnp.dot(pair, stacked, preferred_element_type=jnp.float32)
         fsum = sums[0:8, 0:128] + sums[8:16, 0:128] + sums[0:8, 128:256]
         hsum = sums[0:8, 256:384] + sums[8:16, 256:384] + sums[0:8, 384:512]
         total[tile_rows(target_of(step, u), 2 * ROWS), :] += jnp.concatenate([fsum, hsum], axis=0)
@@ -224,8 +213,7 @@
         lax.fori_loop(0, (listed + GROUP - 1) // GROUP, turn, 0)
 
 
-def finish(state, out_ref):
-    targets, _, centres, total = state
+def finish(targets, centres, totals, out_ref):
     blocks = out_ref.shape[1] // 6
 
     def one(step, carry):
@@ -236,7 +224,11 @@
         ]
         strength = [component(targets, base, 3 + k, ROWS) for k in range(3)]
         fa, fb, ha, hb = [
-            [component(total, wide, start + k, 2 * ROWS) for k in range(3)] for start in (0, 3, 8, 11)
+            [
+                sum(component(total, wide, start + k, 2 * ROWS) for total in totals)
+                for k in range(3)
+            ]
+            for start in (0, 3, 8, 11)
         ]
         swirl = cross(pos, fa)
         lean = cross(strength, fa)
@@ -253,17 +245,10 @@
     lax.fori_loop(0, targets.shape[0] // ROWS // GROUP, one, 0)
 
 
-def fetched(copies):
-    for copy in copies:
-        copy.start()
-    for copy in copies:
-        copy.wait()
-
-
-def sort_list(listed, pair_target, pair_slot, sorted_list, blocks, members):
-    length = pair_target.shape[1]
-    t = pair_target[...]
-    s = pair_slot[...]
+def sort_list(coded, sorted_list, blocks, members):
+    length = coded.shape[1]
+    t = coded[...] // SLOTS
+    s = coded[...] % SLOTS
     t = t - lax.axis_index("across") * blocks
     t = jnp.where(t < 0, t + members * blocks, t)
     partner = jnp.where(lax.axis_index("blk") % 2 == 0, REACH + 1, REACH - 1)
@@ -275,8 +260,7 @@
     kind = jnp.where(
         near, jnp.where(mine, jnp.where(home, 0, 1), 2), jnp.where(mine, 4, 3)
     )
-    entry = lax.broadcasted_iota(jnp.int32, (1, length), 1)
-    kind = jnp.where(entry < listed, kind, CLASSES - 1)
+    kind = jnp.where(coded[...] < 0, CLASSES - 1, kind)
     member = jnp.where(lax.broadcasted_iota(jnp.int32, (CLASSES, length), 0) == kind, 1.0, 0.0)
     row = lax.broadcasted_iota(jnp.int32, (length, length), 0)
     column = lax.broadcasted_iota(jnp.int32, (length, length), 1)
@@ -306,18 +290,16 @@
         return self.ref[pl.ds(pl.multiple_of(rows.start - self.start, ROWS), rows.size), lanes]
 
 
-def home_kernel(number, pair_target, pair_slot, own, *refs, members):
+def home_kernel(coded, own, *refs, members):
     sorted_list, features, centres, total = refs[:4]
-    feature_rows, list_in, slot_in, count_in, lists, sems = refs[4:10]
-    scratch = refs[10:]
+    near_rows, tilt_rows, lists, sems = refs[4:8]
+    scratch = refs[8:]
     state = (own, features, centres, total)
     blocks = own.shape[0] // ROWS
-    pairs = ((number, count_in), (pair_target, list_in), (pair_slot, slot_in))
-    fetched([pltpu.make_async_copy(a, b, sems.at[k]) for k, (a, b) in enumerate(pairs)])
-    sort_list(count_in[0], list_in, slot_in, sorted_list, blocks, members)
-    to_scalars = pltpu.make_async_copy(sorted_list, lists, sems.at[3])
+    sort_list(coded, sorted_list, blocks, members)
+    to_scalars = pltpu.make_async_copy(sorted_list, lists, sems.at[0])
     to_scalars.start()
-    prepare_targets(state, unit_matrix(), feature_rows)
+    prepare_targets(state, near_rows, tilt_rows)
     to_scalars.wait()
     run_class(0, lists, shifted_window(own, REACH * blocks), state, scratch)
 
@@ -329,8 +311,8 @@
 def near_kernel(sorted_list, own, partner, *refs, members):
     others, refs = refs[: members - 1], refs[members - 1 :]
     targets, features, centres, total = state = refs[:4]
-    window, feature_rows, lists, sems = refs[4:8]
-    scratch = refs[8:]
+    window, near_rows, tilt_rows, lists, sems = refs[4:9]
+    scratch = refs[9:]
     to_scalars = pltpu.make_async_copy(sorted_list, lists, sems.at[0])
     to_scalars.start()
     blocks = own.shape[0] // ROWS
@@ -338,21 +320,23 @@
     put_tiles(window, side_of_partner() * blocks, partner)
     for r, other in enumerate(others):
         put_tiles(targets, r * blocks, other)
-    prepare_targets(state, unit_matrix(), feature_rows)
+    prepare_targets(state, near_rows, tilt_rows)
     to_scalars.wait()
     run_class(2, lists, window, state, scratch)
 
 
-def partner_kernel(sorted_list, partner, own, features, centres, _, total, lists, sems, *scratch):
-    fetched([pltpu.make_async_copy(sorted_list, lists, sems.at[0])])
+def partner_kernel(sorted_list, partner, own, features, centres, total, lists, sems, *scratch):
+    to_scalars = pltpu.make_async_copy(sorted_list, lists, sems.at[0])
+    to_scalars.start()
+    total[...] = jnp.zeros_like(total)
+    to_scalars.wait()
     window = shifted_window(partner, side_of_partner() * (partner.shape[0] // ROWS))
     run_class(1, lists, window, (own, features, centres, total), scratch)
 
 
 def far_kernel(sorted_list, paired, passed, crossed, *refs):
-    targets, features, centres, _ = refs[:4]
-    total, window, out_ref = refs[4:7]
-    lists, sems = refs[7:9]
+    targets, features, centres, near_total = refs[:4]
+    window, out_ref, total, lists, sems = refs[4:9]
     scratch = refs[9:]
     state = (targets, features, centres, total)
     to_scalars = pltpu.make_async_copy(sorted_list, lists, sems.at[0])
@@ -363,16 +347,20 @@
     put_tiles(window, jnp.where(even, 2 * REACH, 0) * blocks, paired)
     put_tiles(window, jnp.where(even, 0, 2 * REACH) * blocks, passed)
     put_tiles(window, jnp.where(shard % 2 == 0, REACH - 1, REACH + 1) * blocks, crossed)
+    total[...] = jnp.zeros_like(total)
     to_scalars.wait()
     run_class(3, lists, window, state, scratch)
-    finish(state, out_ref)
-
-
-def last_kernel(sorted_list, window, own, features, centres, _, total, out_ref, lists, sems, *scratch):
-    state = (own, features, centres, total)
-    fetched([pltpu.make_async_copy(sorted_list, lists, sems.at[0])])
-    run_class(4, lists, window, state, scratch)
-    finish(state, out_ref)
+    finish(targets, centres, (near_total, total), out_ref)
+
+
+def last_kernel(sorted_list, window, own, features, centres, *refs):
+    home_total, partner_total, out_ref, total, lists, sems = refs[:6]
+    to_scalars = pltpu.make_async_copy(sorted_list, lists, sems.at[0])
+    to_scalars.start()
+    total[...] = jnp.zeros_like(total)
+    to_scalars.wait()
+    run_class(4, lists, window, (own, features, centres, total), refs[6:])
+    finish(own, centres, (home_total, partner_total, total), out_ref)
 
 
 def section_kernel(own, sums, *refs):
@@ -390,17 +378,15 @@
             stepped[:, lanes] = own[first : first + 3, :] + section_step * value
 
 
-def call(kernel, name, inputs, outputs, scratch, aliases=None, far=0, flops=0):
+def call(kernel, name, inputs, outputs, scratch, flops=0):
     vmem = pl.BlockSpec(memory_space=pltpu.VMEM)
-    hbm = pl.BlockSpec(memory_space=pltpu.HBM)
     held = sum(value.size * value.dtype.itemsize for value in (*inputs, *outputs))
     return pl.pallas_call(
         kernel,
         out_shape=outputs,
-        in_specs=[hbm if k < far else vmem for k in range(len(inputs))],
+        in_specs=[vmem for value in inputs],
         out_specs=[vmem for value in outputs],
         scratch_shapes=scratch,
-        input_output_aliases=aliases or {},
         compiler_params=pltpu.CompilerParams(vmem_limit_bytes=10 * 1024 * 1024 + 2 * held),
         cost_estimate=pl.CostEstimate(flops=flops, bytes_accessed=0, transcendentals=0),
         name=name,
@@ -418,16 +404,15 @@
     def f32(*shape):
         return jax.ShapeDtypeStruct(shape, jnp.float32)
 
-    slot_index = lax.broadcasted_iota(jnp.int32, (blocks, 3, BLOCK), 2)
-    live = jnp.where(
-        slot_index < block_count[:, None, None],
-        strengths.reshape(3, blocks, BLOCK).transpose(1, 0, 2),
-        0.0,
-    )
+    row = lax.broadcasted_iota(jnp.int32, (blocks, ROWS, BLOCK), 1)
+    lane = lax.broadcasted_iota(jnp.int32, (blocks, ROWS, BLOCK), 2)
     cores = radius.reshape(blocks, 1, BLOCK)
-    own = jnp.concatenate(
-        [positions.reshape(3, blocks, BLOCK).transpose(1, 0, 2), live, cores, cores], axis=1
-    ).reshape(blocks * ROWS, BLOCK)
+    parts = [value.reshape(3, blocks, BLOCK).transpose(1, 0, 2) for value in (positions, strengths)]
+    dead = (row >= 3) & (row < 6) & (lane >= block_count[:, None, None])
+    own = jnp.where(dead, 0.0, jnp.concatenate(parts + [cores, cores], axis=1))
+    own = own.reshape(blocks * ROWS, BLOCK)
+    entry = lax.broadcasted_iota(jnp.int32, (1, length), 1)
+    coded = jnp.where(entry < pair_count[0], pair_target * SLOTS + pair_slot, -1)
     paired = moved(own, "blk", to_paired_chip)
     others = [
         moved(own, "across", lambda source: (source - away) % members) for away in range(1, members)
@@ -437,7 +422,7 @@
     def state_shapes(number):
         return [
             f32(number * blocks * ROWS, BLOCK),
-            jax.ShapeDtypeStruct((number * blocks, BLOCK, FEATURES), jnp.bfloat16),
+            jax.ShapeDtypeStruct((number * blocks, FEATURES, 2 * BLOCK), jnp.bfloat16),
             f32(number * blocks * ROWS, BLOCK),
             f32(number * blocks * 2 * ROWS, BLOCK),
         ]
@@ -445,11 +430,11 @@
     own_shapes, other_shapes = state_shapes(1), state_shapes(members - 1)
     window_shape = f32((2 * REACH + 1) * blocks * ROWS, BLOCK)
     list_shape = jax.ShapeDtypeStruct((3 * ROWS * length // BLOCK, BLOCK), jnp.int32)
-    feature_rows = pltpu.VMEM((GROUP * BLOCK, BLOCK), jnp.float32)
+    feature_rows = [pltpu.VMEM((GROUP * FEATURES, BLOCK), jnp.float32)] * 2
     list_scratch = [pltpu.SMEM(list_shape.shape, jnp.int32), pltpu.SemaphoreType.DMA((4,))]
     scratch = [
         pltpu.VMEM((GROUP * ROWS, BLOCK), jnp.float32),
-        pltpu.VMEM((GROUP * 32, BLOCK), jnp.float32),
+        pltpu.VMEM((GROUP * FEATURES, BLOCK), jnp.float32),
         pltpu.VMEM((GROUP * 2 * ROWS, BLOCK), jnp.float32),
         pltpu.VMEM((GROUP * 2 * ROWS, BLOCK), jnp.bfloat16),
         pltpu.VMEM((HALF, BLOCK, 2 * BLOCK), jnp.float32),
@@ -460,17 +445,9 @@
     lists, *own_state = call(
         lambda *refs: home_kernel(*refs, members=members),
         "home_pairs",
-        (pair_count, pair_target, pair_slot, own),
+        (coded, own),
         [list_shape] + own_shapes[1:],
-        [
-            feature_rows,
-            pltpu.VMEM((1, length), jnp.int32),
-            pltpu.VMEM((1, length), jnp.int32),
-            pltpu.SMEM((1,), jnp.int32),
-        ]
-        + list_scratch
-        + scratch,
-        far=3,
+        feature_rows + list_scratch + scratch,
         flops=HOME_FLOPS,
     )
     paired, lists = lax.optimization_barrier((paired, lists))
@@ -480,43 +457,40 @@
         "near_pairs",
         (lists, own, partner, *others),
         other_shapes,
-        [window_scratch, feature_rows] + list_scratch + scratch,
+        [window_scratch] + feature_rows + list_scratch + scratch,
         flops=NEAR_FLOPS,
     ))
     passed, other_state[3] = lax.optimization_barrier((passed, other_state[3]))
     core = shard % 2
     chip = shard // 2 % 2
     crossed = moved(jnp.where(core == chip, paired, passed), "blk", to_other_core)
-    (own_state[2],) = call(
+    (partner_total,) = call(
         partner_kernel,
         "partner_pairs",
-        (lists, partner, own, *own_state),
+        (lists, partner, own, *own_state[:2]),
         [own_shapes[3]],
         list_scratch + scratch,
-        {5: 0},
         flops=HOME_FLOPS,
     )
-    crossed, own_state[2] = lax.optimization_barrier((crossed, own_state[2]))
-    _, window, away_sums = call(
+    crossed, partner_total = lax.optimization_barrier((crossed, partner_total))
+    window, away_sums = call(
         far_kernel,
         "far_pairs",
         (lists, paired, passed, crossed, *other_state),
-        [other_shapes[3], window_shape, f32(members - 1, 6 * blocks, BLOCK)],
-        list_scratch + scratch,
-        {7: 0},
+        [window_shape, f32(members - 1, 6 * blocks, BLOCK)],
+        [pltpu.VMEM(other_shapes[3].shape, jnp.float32)] + list_scratch + scratch,
         flops=FAR_FLOPS,
     )
     returned = [
         moved(away_sums[away - 1], "across", lambda source: (source + away) % members)
         for away in range(1, members)
     ]
-    _, sums = call(
+    (sums,) = call(
         last_kernel,
         "last_pairs",
-        (lists, window, own, *own_state),
-        [own_shapes[3], f32(1, 6 * blocks, BLOCK)],
-        list_scratch + scratch,
-        {5: 0},
+        (lists, window, own, *own_state, partner_total),
+        [f32(1, 6 * blocks, BLOCK)],
+        [pltpu.VMEM(own_shapes[3].shape, jnp.float32)] + list_scratch + scratch,
         flops=FAR_FLOPS,
     )
     wide = f32(3, lanes)

time: 47.9 us -> 44.3 us (0.925)
  the two profiles are of different devices: /device:TPU:0 before, /device:TPU:29 now
where the time goes in v5:
time: 44.3 us; the launch traced here: 43.5 us
  Pallas kernels  30.1 us (68%)
  starting transfers between devices  4.69 us (11%)
  waiting for transfers between devices  4.4 us (10%)
  other arithmetic  1.96 us (4%)
  between operations  1.4 us (3%)
  local copies, waits for them, and re-layouts  0.92 us (2%)
    pallas_call x6, Pallas kernels, call(): pl.pallas_call(kernel, out_shape=outputs, in_specs=[vmem for value in inp...  30.1 us
    ppermute x6, starting transfers between devices, moved(): return lax.ppermute(value, axis, pairs)  4.69 us
    ppermute x6, waiting for transfers between devices, moved(): return lax.ppermute(value, axis, pairs)  4.4 us
    select_n x1, other arithmetic, shards(): own = jnp.where(dead, 0.0, jnp.concatenate(parts + [cores, cores], axis=1))  1.21 us
  transfers between devices with their start and end apart: 6, of which 2 were waited for; matrix products, arithmetic and copies ran while one was open for 2% of the time, Pallas kernels for 49%

profile of v5, /device:TPU:29, one launch (start us, length us, event | category | flops | bytes accessed | tf_op | source)
XLA Modules:
  0.0 43.5 jit_solution(18429333151716710292)
XLA Ops:
  0.7 0.1 and.29
  0.8 0.7 %ge.22 = s32[64,8]{1,0:T(8,128)S(1)} broadcast(s32[64]{0:T(128)} %param.10), dimensions={0} | broadcast | bytes 2304 | tf_op jit(solution)/shard_map/ge | solution.py:411
  1.5 0.1 ge.23
  1.6 1.2 %fusion.refs_1_.own = f32[512,128]{1,0:T(8,128)S(1)} fusion(f32[64,1,128]{2,1,0:T(1,128)} %bitcast.19, f32[64,3,128]{2,1,0:T(4,128)} %bitcast.17, f32[64,3,128]{2,1,0:T(4,128)} %bitcast.18, s32[512]{0:T(512)S(1)} %ge.23, pred[512]{0:T(512)(128)(4,1)S(1)} %and.29), kind=kLoop, calls=%fused_computation.1 | loop fusion | flops 393216 | bytes 494080 | tf_op jit(solution)/shard_map/jit(_where)/select_n | solution.py:412
  2.8 1.3 %collective-permute-start.3 = (f32[512,128]{1,0:T(8,128)S(1)}, f32[512,128]{1,0:T(8,128)S(1)}, u32[]{:S(2)}, u32[]{:S(2)}) collective-permute-start(f32[512,128]{1,0:T(8,128)S(1)} %fusion.refs_1_.own), channel_id=1, source_target_pairs={{0,1},{1,0},{2,3},{3,2},{4,5},{5,4},{6,7},{7,6},{8,9},{9,8},{10,11... | collective-permute-start | bytes 786440 | tf_op jit(solution)/shard_map/ppermute | solution.py:23
  4.1 1.0 %collective-permute-start.2 = (f32[512,128]{1,0:T(8,128)S(1)}, f32[512,128]{1,0:T(8,128)S(1)}, u32[]{:S(2)}, u32[]{:S(2)}) collective-permute-start(f32[512,128]{1,0:T(8,128)S(1)} %fusion.refs_1_.own), channel_id=1, source_target_pairs={{0,2},{2,0},{4,6},{6,4},{8,10},{10,8},{12,14},{14,12},{16,18},{18,... | collective-permute-start | bytes 786440 | tf_op jit(solution)/shard_map/ppermute | solution.py:23
  5.0 0.2 collective-permute-start
  5.9 0.7 %compare_select_fusion.refs_0_ = s32[1,256]{1,0:T(1,128)S(1)} fusion(s32[1,256]{1,0:T(1,128)} %param.12, s32[1,256]{1,0:T(1,128)} %param.11, s32[]{:T(128)} %bitcast.14), kind=kLoop, calls=%fused_computation.5 | loop fusion | flops 1024 | bytes 3076 | tf_op jit(solution)/shard_map/jit(_where)/select_n | solution.py:415
  6.6 4.5 %home_pairs.1 = (s32[48,128]{1,0:T(8,128)S(1)}, bf16[64,32,256]{2,1,0:T(8,128)(2,1)S(1)}, f32[512,128]{1,0:T(8,128)S(1)}, f32[1024,128]{1,0:T(8,128)S(1)}) custom-call(s32[1,256]{1,0:T(1,128)S(1)} %compare_select_fusion.refs_0_, f32[512,128]{1,0:T(8,128)S(1)} %fusion.refs_1_.own), custom_call_target="tpu_custom_call" | custom-call | flops 10000000000 | tf_op jit(solution)/shard_map/home_pairs/pallas_call | solution.py:384
  11.2 1.8 %collective-permute-done.paired = f32[512,128]{1,0:T(8,128)S(1)} collective-permute-done((f32[512,128]{1,0:T(8,128)S(1)}, f32[512,128]{1,0:T(8,128)S(1)}, u32[]{:S(2)}, u32[]{:S(2)}) %collective-permute-start) | collective-permute-done | bytes 262176 | tf_op jit(solution)/shard_map/ppermute | solution.py:23
  13.0 0.2 collective-permute-start.1
  13.1 0.0 collective-permute-done.3.refs_3_
  13.1 0.0 collective-permute-done.2.refs_2_.partner
  13.1 6.0 %near_pairs.1 = (f32[512,128]{1,0:T(8,128)S(1)}, bf16[64,32,256]{2,1,0:T(8,128)(2,1)S(1)}, f32[512,128]{1,0:T(8,128)S(1)}, f32[1024,128]{1,0:T(8,128)S(1)}) custom-call(s32[48,128]{1,0:T(8,128)S(1)} %get-tuple-element.21.refs_0_.sorted_list, f32[512,128]{1,0:T(8,128)S(1)} %fusion.refs_1_.own, f32[512,128]{1,0:T(8,128)S(1)} %collective-permute-done.2.refs_2_.partner, ...), custom_call_target="tpu_custom_call" | custom-call | flops 10000000000 | tf_op jit(solution)/shard_map/near_pairs/pallas_call | solution.py:384
  19.2 2.6 %collective-permute-done.1.passed = f32[512,128]{1,0:T(8,128)S(1)} collective-permute-done((f32[512,128]{1,0:T(8,128)S(1)}, f32[512,128]{1,0:T(8,128)S(1)}, u32[]{:S(2)}, u32[]{:S(2)}) %collective-permute-start.1) | collective-permute-done | bytes 262176 | tf_op jit(solution)/shard_map/ppermute | solution.py:23
  21.8 1.7 %collective-permute-start.4 = (f32[512,128]{1,0:T(8,128)S(1)}, f32[512,128]{1,0:T(8,128)S(1)}, u32[]{:S(2)}, u32[]{:S(2)}) collective-permute-start(f32[512,128]{1,0:T(8,128)S(1)} %broadcast_select_fusion), channel_id=1, source_target_pairs={{0,2},{2,0},{4,6},{6,4},{8,10},{10,8},{12,14},{14,12},{16,18},{18,... | collective-permute-start | bytes 786440 | tf_op jit(solution)/shard_map/ppermute | solution.py:23
  23.6 3.1 %partner_pairs.1.refs_1_ = f32[1024,128]{1,0:T(8,128)S(1)} custom-call(s32[48,128]{1,0:T(8,128)S(1)} %get-tuple-element.21.refs_0_.sorted_list, f32[512,128]{1,0:T(8,128)S(1)} %collective-permute-done.2.refs_2_.partner, f32[512,128]{1,0:T(8,128)S(1)} %fusion.refs_1_.own, bf16[64,32,256]{2,1,0:T(8,128)(2,1)S(1)} %get-tuple-element.25.features, ...), custom_call_target="tpu_custom_call" | custom-call | flops 10000000000 | tf_op jit(solution)/shard_map/partner_pairs/pallas_call | solution.py:384
  26.7 0.0 collective-permute-done.4.crossed
  26.8 7.6 %far_pairs.1 = (f32[2560,128]{1,0:T(8,128)S(1)}, f32[1,384,128]{2,1,0:T(8,128)S(1)}) custom-call(s32[48,128]{1,0:T(8,128)S(1)} %get-tuple-element.21.refs_0_.sorted_list, f32[512,128]{1,0:T(8,128)S(1)} %collective-permute-done.paired, f32[512,128]{1,0:T(8,128)S(1)} %collective-permute-done.1.passed, f32[512,128]{1,0:T(8,128)S(1)} %collective-permute-done.4.crossed, ...), custom_call_target="tpu_custom_call" | custom-call | flops 10000000000 | tf_op jit(solution)/shard_map/far_pairs/pallas_call | solution.py:384
  34.4 0.3 collective-permute-start.5
  34.7 7.6 %last_pairs.1 = f32[1,384,128]{2,1,0:T(8,128)S(1)} custom-call(s32[48,128]{1,0:T(8,128)S(1)} %get-tuple-element.21.refs_0_.sorted_list, f32[2560,128]{1,0:T(8,128)S(1)} %get-tuple-element.32.window, f32[512,128]{1,0:T(8,128)S(1)} %fusion.refs_1_.own, bf16[64,32,256]{2,1,0:T(8,128)(2,1)S(1)} %get-tuple-element.25.features, ...), custom_call_target="tpu_custom_call" | custom-call | flops 10000000000 | tf_op jit(solution)/shard_map/last_pairs/pallas_call | solution.py:384
  42.3 0.0 collective-permute-done.5.refs_0_
  42.4 1.1 %section.1 = (f32[3,8192]{1,0:T(4,128)}, f32[3,8192]{1,0:T(4,128)}, f32[3,8192]{1,0:T(4,128)}, f32[3,8192]{1,0:T(4,128)}) custom-call(f32[512,128]{1,0:T(8,128)S(1)} %fusion.refs_1_.own, f32[384,128]{1,0:T(8,128)S(1)} %bitcast.15, f32[384,128]{1,0:T(8,128)S(1)} %collective-permute-done.5.refs_0_), custom_call_target="tpu_custom_call" | custom-call | tf_op jit(solution)/shard_map/section/pallas_call | solution.py:384
  (3 shorter events, 0.0 us)
Async XLA Ops:
  2.8 10.3 %collective-permute-start.3 = (f32[512,128]{1,0:T(8,128)S(1)}, f32[512,128]{1,0:T(8,128)S(1)}, u32[]{:S(2)}, u32[]{:S(2)}) collective-permute-start(f32[512,128]{1,0:T(8,128)S(1)} %fusion.refs_1_.own), channel_id=1, source_target_pairs={{0,1},{1,0},{2,3},{3,2},{4,5},{5,4},{6,7},{7,6},{8,9},{9,8},{10,11... | collective-permute-start | bytes 786440 | tf_op jit(solution)/shard_map/ppermute | solution.py:23
  4.1 9.1 %collective-permute-start.2 = (f32[512,128]{1,0:T(8,128)S(1)}, f32[512,128]{1,0:T(8,128)S(1)}, u32[]{:S(2)}, u32[]{:S(2)}) collective-permute-start(f32[512,128]{1,0:T(8,128)S(1)} %fusion.refs_1_.own), channel_id=1, source_target_pairs={{0,2},{2,0},{4,6},{6,4},{8,10},{10,8},{12,14},{14,12},{16,18},{18,... | collective-permute-start | bytes 786440 | tf_op jit(solution)/shard_map/ppermute | solution.py:23
  5.0 7.9 %collective-permute-start = (f32[512,128]{1,0:T(8,128)S(1)}, f32[512,128]{1,0:T(8,128)S(1)}, u32[]{:S(2)}, u32[]{:S(2)}) collective-permute-start(f32[512,128]{1,0:T(8,128)S(1)} %fusion.refs_1_.own), channel_id=1, source_target_pairs={{0,4},{2,6},{4,0},{6,2},{8,12},{10,14},{12,8},{14,10},{16,20},{18,... | collective-permute-start | bytes 786440 | tf_op jit(solution)/shard_map/ppermute | solution.py:23
  13.0 8.8 %collective-permute-start.1 = (f32[512,128]{1,0:T(8,128)S(1)}, f32[512,128]{1,0:T(8,128)S(1)}, u32[]{:S(2)}, u32[]{:S(2)}) collective-permute-start(f32[512,128]{1,0:T(8,128)S(1)} %collective-permute-done.paired), channel_id=1, source_target_pairs={{0,8},{2,10},{4,28},{6,30},{8,16},{10,18},{12,4},{14,6},{16,24},{1... | collective-permute-start | bytes 786440 | tf_op jit(solution)/shard_map/ppermute | solution.py:23
  21.8 4.9 %collective-permute-start.4 = (f32[512,128]{1,0:T(8,128)S(1)}, f32[512,128]{1,0:T(8,128)S(1)}, u32[]{:S(2)}, u32[]{:S(2)}) collective-permute-start(f32[512,128]{1,0:T(8,128)S(1)} %broadcast_select_fusion), channel_id=1, source_target_pairs={{0,2},{2,0},{4,6},{6,4},{8,10},{10,8},{12,14},{14,12},{16,18},{18,... | collective-permute-start | bytes 786440 | tf_op jit(solution)/shard_map/ppermute | solution.py:23
  34.4 8.0 %collective-permute-start.5 = (f32[384,128]{1,0:T(8,128)S(1)}, f32[384,128]{1,0:T(8,128)S(1)}, u32[]{:S(2)}, u32[]{:S(2)}) collective-permute-start(f32[384,128]{1,0:T(8,128)S(1)} %bitcast.16), channel_id=1, source_target_pairs={{0,1},{1,0},{2,3},{3,2},{4,5},{5,4},{6,7},{7,6},{8,9},{9,8},{10,11... | collective-permute-start | bytes 589832 | tf_op jit(solution)/shard_map/ppermute | solution.py:23
